TPU v7x, 128 devices: a whole 4x4x4 slice. The times are simulated.
128 devices in a mesh: rows: 16 (over y, x), cols: 8 (over z, core).
Axes of the slice: x: 4, y: 4, z: 4, core: 2. Of those that a mesh axis runs over, the one named last changes fastest.
Arguments:
- node_features: float32 [98304, 256], P(('rows', 'cols')), may hold values from -24 to 24
- cotangent: float32 [98304, 256], P(('rows', 'cols')), may hold values from -6 to 6
- w_query: float32 [256, 256], replicated, may hold values from -0.375 to 0.375
- w_key: float32 [256, 256], replicated, may hold values from -0.375 to 0.375
- w_value: float32 [256, 256], replicated, may hold values from -0.375 to 0.375
- w_graph: float32 [256, 256], replicated, may hold values from -0.375 to 0.375
- tile_values: float32 [36864, 128, 128], P(('rows', 'cols')), may hold values from -0.078125 to 0.078125
- tile_rows: int32 [36864], P(('rows', 'cols')), may hold values from 0 to 47, as said below
- tile_cols: int32 [36864], P(('rows', 'cols')), may hold values from 0 to 95
- tile_count: int32 [128], P(('rows', 'cols')), may hold values from 36 to 288, as said below
Outputs:
- output: float32 [98304, 256], P(('rows', 'cols'))
- grad_x: float32 [98304, 256], P(('rows', 'cols'))
- grad_query: float32 [256, 256], replicated
- grad_key: float32 [256, 256], replicated
- grad_value: float32 [256, 256], replicated
- grad_graph: float32 [256, 256], replicated
Inputs may be any that keep to these rules, and one draw needn't show every extreme that they name: The (tile_rows, tile_cols) pairs of one device's 288 slots are all different; slots past a device's count hold data that is not part of A. `tile_count`: some device has all 288 slots live and some device only 36.
All inputs are finite; a program needn't handle non-finite values.
Results may differ from a plain program's by a relative error of at most 0.0003.
Values sent between devices are 32-bit elements; how exact they have to be, the bound alone decides.
A program may use at most 192 MiB of HBM per device.

v0:
```python
import jax
import jax.numpy as jnp
from jax import lax
from jax.sharding import PartitionSpec as P

TILE = 128


def hi_dot(left, right):
    return jnp.dot(left, right, precision=lax.Precision.HIGHEST)


def elu_slope(inputs):
    return jnp.where(inputs > 0, 1.0, jnp.exp(jnp.minimum(inputs, 0.0)))


def tile_sum(tile_values, row_list, col_list, tile_total, source, out_blocks, transpose):
    width = source.shape[1]
    source_blocks = source.reshape(-1, TILE, width)
    slot_ids = jnp.arange(8, dtype=jnp.int32)

    def add_block(block_index, running):
        first_slot = block_index * 8
        block_values = lax.dynamic_slice_in_dim(tile_values, first_slot, 8, 0)
        row_ids = lax.dynamic_slice_in_dim(row_list, first_slot, 8, 0)
        col_ids = lax.dynamic_slice_in_dim(col_list, first_slot, 8, 0)
        alive_mask = (first_slot + slot_ids < tile_total).astype(jnp.float32)
        if transpose:
            picked = source_blocks[row_ids]
            product = jnp.einsum(
                "tji,tjd->tid", block_values, picked, precision=lax.Precision.HIGHEST
            )
            placing_ids = col_ids
        else:
            picked = source_blocks[col_ids]
            product = jnp.einsum(
                "tij,tjd->tid", block_values, picked, precision=lax.Precision.HIGHEST
            )
            placing_ids = row_ids
        return running.at[placing_ids].add(product * alive_mask[:, None, None])

    empty = jnp.zeros((out_blocks, TILE, width), jnp.float32)
    running = lax.fori_loop(0, (tile_total + 7) // 8, add_block, empty)
    return running.reshape(out_blocks * TILE, width)


def per_device(
    node_features,
    cotangent,
    w_query,
    w_key,
    w_value,
    w_graph,
    tile_values,
    tile_rows,
    tile_cols,
    tile_count,
):
    row_devices = lax.axis_size("rows")
    col_devices = lax.axis_size("cols")
    node_rows = node_features.shape[0]
    tile_total = tile_count[0]
    panel_source = hi_dot(node_features, w_graph)
    panel = lax.all_gather(panel_source, "rows", axis=0, tiled=True)
    query = hi_dot(node_features, w_query)
    key_proj = hi_dot(node_features, w_key)
    value_proj = hi_dot(node_features, w_value)
    feat_q = jax.nn.elu(query) + 1.0
    feat_k = jax.nn.elu(key_proj) + 1.0
    state, key_sum = lax.psum(
        (hi_dot(feat_k.T, value_proj), jnp.sum(feat_k, axis=0)), ("rows", "cols")
    )
    partial_rows = tile_sum(
        tile_values, tile_rows, tile_cols, tile_total, panel, node_rows * col_devices // TILE, False
    )
    gathered_rows = lax.psum_scatter(partial_rows, "cols", scatter_dimension=0, tiled=True)
    denominator = hi_dot(feat_q, key_sum)
    attended = hi_dot(feat_q, state) / denominator[:, None]
    output = attended + gathered_rows
    scaled = cotangent / denominator[:, None]
    weight_dot = jnp.sum(cotangent * attended, axis=1) / denominator
    grad_feat_q = hi_dot(scaled, state.T) - weight_dot[:, None] * key_sum[None, :]
    grad_state, grad_key_sum = lax.psum(
        (hi_dot(feat_q.T, scaled), -hi_dot(weight_dot, feat_q)), ("rows", "cols")
    )
    grad_feat_k = hi_dot(value_proj, grad_state.T) + grad_key_sum[None, :]
    grad_values = hi_dot(feat_k, grad_state)
    grad_query_proj = grad_feat_q * elu_slope(query)
    grad_keys = grad_feat_k * elu_slope(key_proj)
    local_query = hi_dot(node_features.T, grad_query_proj)
    local_key = hi_dot(node_features.T, grad_keys)
    local_value = hi_dot(node_features.T, grad_values)
    grad_query, grad_key, grad_value = lax.psum(
        (local_query, local_key, local_value), ("rows", "cols")
    )
    grad_x = (
        hi_dot(grad_query_proj, w_query.T)
        + hi_dot(grad_keys, w_key.T)
        + hi_dot(grad_values, w_value.T)
    )
    row_cotangent = lax.all_gather(cotangent, "cols", axis=0, tiled=True)
    column_terms = tile_sum(
        tile_values,
        tile_rows,
        tile_cols,
        tile_total,
        row_cotangent,
        node_rows * row_devices // TILE,
        True,
    )
    returned = lax.psum_scatter(column_terms, "rows", scatter_dimension=0, tiled=True)
    grad_x = grad_x + hi_dot(returned, w_graph.T)
    local_graph = hi_dot(node_features.T, returned)
    grad_graph = lax.psum(local_graph, ("rows", "cols"))
    return (output, grad_x, grad_query, grad_key, grad_value, grad_graph)


def solution(mesh):
    in_specs = (
        P(("rows", "cols"), None),
        P(("rows", "cols"), None),
        P(),
        P(),
        P(),
        P(),
        P(("rows", "cols"), None, None),
        P(("rows", "cols")),
        P(("rows", "cols")),
        P(("rows", "cols")),
    )
    out_specs = (P(("rows", "cols"), None), P(("rows", "cols"), None), P(), P(), P(), P())
    return jax.shard_map(
        per_device, mesh=mesh, in_specs=in_specs, out_specs=out_specs, check_vma=False
    )
```

profile of v0, /device:TPU:1, one launch (start us, length us, event | category | flops | bytes accessed | tf_op | source)
XLA Modules:
  0.0 1138.8 jit_solution(10012282581194724918)
XLA Ops:
  16.2 70.4 %psum.57 = f32[256]{0:T(256)S(1)} all-reduce(f32[256]{0:T(256)S(1)} %get-tuple-element.200), channel_id=1, replica_groups=mesh['rows'=16,'cols'=8] {'rows','cols'}, use_global_device_ids=true, to_apply=%region_2.3 | all-reduce | flops 256 | bytes 2048 | tf_op jit(solution)/shard_map/psum | solution.py:70
  97.5 9.0 all-gather.3.cloned.1.call-done
  109.9 205.0 %while.22 = (s32[]{:T(128)}, f32[48,128,256]{2,1,0:T(8,128)}, s32[]{:T(128)}, s32[288]{0:T(512)S(1)}, f32[288,128,128]{2,1,0:T(8,128)}, /*index=5*/s32[288]{0:T(...) while((s32[]{:T(128)}, f32[48,128,256]{2,1,0:T(8,128)}, ...), condition=%wide.region_5.6_spmd.clone, body=%wide.region_3.5_spmd.clone.sunk | while | flops 403178560 | bytes 7868891 | solution.py:43
  110.1 5.3 gather_fusion
  121.7 5.3 gather_fusion
  133.2 5.4 gather_fusion
  144.8 5.3 gather_fusion
  156.3 5.2 gather_fusion
  167.6 5.2 gather_fusion
  178.9 5.2 gather_fusion
  201.6 5.2 gather_fusion
  212.9 5.2 gather_fusion
  224.3 5.2 gather_fusion
  235.7 5.2 gather_fusion
  247.1 5.2 gather_fusion
  281.0 5.2 gather_fusion
  292.4 5.2 gather_fusion
  303.7 5.2 gather_fusion
  314.9 6.6 copy.25
  321.6 6.1 broadcast_in_dim.32
  327.7 173.4 %while.23 = (s32[]{:T(128)}, f32[96,128,256]{2,1,0:T(8,128)}, s32[]{:T(128)}, s32[288]{0:T(512)S(1)}, f32[288,128,128]{2,1,0:T(8,128)}, /*index=5*/s32[288]{0:T(...) while((s32[]{:T(128)}, f32[96,128,256]{2,1,0:T(8,128)}, ...), condition=%wide.region_12.13_spmd.clone, body=%wide.region_10.12_spmd.clone.sunk | while | flops 403178560 | bytes 7868891 | solution.py:43
  506.3 60.9 %reduce-scatter.3.cloned.1.call-done = f32[768,256]{0,1:T(8,128)} async-done(((f32[6144,256]{0,1:T(8,128)}), f32[768,256]{0,1:T(8,128)}) %reduce-scatter.3.cloned.1.call-update) | async-done | bytes 786448 | tf_op jit(solution)/shard_map/reduce_scatter | solution.py:76
  575.2 384.1 %psum.59 = f32[256]{0:T(256)S(1)} all-reduce(f32[256]{0:T(256)S(1)} %neg.3), channel_id=1, replica_groups=mesh['rows'=16,'cols'=8] {'rows','cols'}, use_global_device_ids=true, to_apply=%region_9.10 | all-reduce | flops 256 | bytes 2048 | tf_op jit(solution)/shard_map/psum | solution.py:83
  981.9 142.6 %all-reduce.5.cloned.1.call-done = (f32[256,256]{0,1:T(8,128)}, f32[256,256]{0,1:T(8,128)}, f32[256,256]{0,1:T(8,128)}, f32[256,256]{0,1:T(8,128)}) async-done(((f32[256,256]{0,1:T(8,128)}, f32[256,256]{0,1:T(8,128)}, f32[256,256]{0,1:T(8,128)}, f32[256,256]{0,1:T(8,128)}), (f32[256,256]{0,1:T(8,128)}, f32[256,256]{0,1:T(8,128)}, f32[256,256]{0,1:T(8,128)}, ...) | async-done | bytes 1048592 | tf_op jit(solution)/shard_map/psum | solution.py:93
  (270 shorter events, 363.6 us)
Async XLA Ops:
  8.0 1.1 copy-start
  8.0 101.9 %copy-start.10 = (s32[288]{0:T(512)S(1)}, s32[288]{0:T(512)}, u32[]{:S(2)}) copy-start(s32[288]{0:T(512)} %param.21) | copy-start | bytes 3460
  8.0 101.9 %copy-start.11 = (s32[288]{0:T(512)S(1)}, s32[288]{0:T(512)}, u32[]{:S(2)}) copy-start(s32[288]{0:T(512)} %param.22) | copy-start | bytes 3460
  8.0 98.5 %all-gather.3.cloned.1.call-start = ((), (), s32[]{:S(2)}) async-start(), calls=%async_computation.2 | async-start | bytes 13369344 | tf_op jit(solution)/shard_map/all_gather | solution.py:64
  11.8 309.8 %all-gather.5.cloned.1.call-start = ((), (), s32[]{:S(2)}) async-start(), calls=%async_computation.4 | async-start | bytes 7077888 | tf_op jit(solution)/shard_map/all_gather | solution.py:101
  12.5 488.7 %all-reduce.7.cloned.1.call-start = ((), (), s32[]{:S(2)}) async-start(), calls=%async_computation.7 | async-start | bytes 1048576 | tf_op jit(solution)/shard_map/psum | solution.py:70
  14.0 96.0 %copy-start.9 = (f32[768,256]{0,1:T(8,128)}, f32[768,256]{0,1:T(8,128)S(1)}, u32[]{:S(2)}) copy-start(f32[768,256]{0,1:T(8,128)S(1)} %copy.17) | copy-start | bytes 2359300
  16.2 93.8 %copy-start.1 = (f32[768,256]{1,0:T(8,128)}, f32[768,256]{1,0:T(8,128)S(1)}, u32[]{:S(2)}) copy-start(f32[768,256]{1,0:T(8,128)S(1)} %get-tuple-element.201) | copy-start | bytes 2359300
  88.3 6.0 copy-start.8
  91.1 0.9 copy-start.3
  96.8 470.5 %reduce-scatter.3.cloned.1.call-start = ((), (), s32[]{:S(2)}) async-start(), calls=%async_computation.3 | async-start | bytes 7077888 | tf_op jit(solution)/shard_map/reduce_scatter | solution.py:76
  321.5 652.5 %reduce-scatter.5.cloned.1.call-start = ((), (), s32[]{:S(2)}) async-start(), calls=%async_computation.5 | async-start | bytes 13369344 | tf_op jit(solution)/shard_map/reduce_scatter | solution.py:111
  501.1 1.1 copy-start.2
  501.1 461.2 %copy-start.5 = (f32[256,256]{1,0:T(8,128)S(1)}, f32[256,256]{1,0:T(8,128)}, u32[]{:S(2)}) copy-start(f32[256,256]{1,0:T(8,128)} %param.16) | copy-start | bytes 786436
  501.1 464.1 %copy-start.4 = (f32[768,256]{1,0:T(8,128)S(1)}, f32[768,256]{1,0:T(8,128)}, u32[]{:S(2)}) copy-start(f32[768,256]{1,0:T(8,128)} %copy-done.3) | copy-start | bytes 2359300
  501.1 623.4 %all-reduce.5.cloned.1.call-start = ((), (), s32[]{:S(2)}) async-start(), calls=%async_computation.6 | async-start | bytes 2097152 | tf_op jit(solution)/shard_map/psum | solution.py:93
  959.2 9.9 copy-start.6
  963.1 16.0 %copy-start.7 = (f32[256,256]{1,0:T(8,128)S(1)}, f32[256,256]{1,0:T(8,128)}, u32[]{:S(2)}) copy-start(f32[256,256]{1,0:T(8,128)} %param.19) | copy-start | bytes 786436
Sparse Core Ops, SparseCore 0:
  11.9 94.5 all-gather.2
  108.2 41.0 all-gather.4
  321.7 245.5 reduce-scatter.2
  570.9 403.0 reduce-scatter.4
Sparse Core Ops, SparseCore 1:
  96.9 156.3 all-reduce.6
  977.4 147.1 all-reduce.4
where the time goes:
time: 1150 us; the launch traced here: 1140 us
  blocking collectives  454 us (39%)
  waiting for transfers between devices  217 us (19%)
  local copies, waits for them, and re-layouts  185 us (16%)
  other arithmetic  147 us (13%)
  matrix products  118 us (10%)
  between operations  16.1 us (1%)
    psum x1, blocking collectives, per_device(): lax.psum((hi_dot(feat_q.T, scaled), -hi_dot(weight_dot, feat_q)), ('rows'...  384 us
    psum x1, waiting for transfers between devices, per_device(): lax.psum((local_query, local_key, local_value), ('rows', 'cols'))  143 us
    scatter-add x36, other arithmetic, add_block(): return running.at[placing_ids].add(product * alive_mask[:, None, None])  120 us
    gather x18, local copies, waits for them, and re-layouts, add_block(): picked = source_blocks[col_ids]  94.1 us
    psum x1, blocking collectives, per_device(): lax.psum((hi_dot(feat_k.T, value_proj), jnp.sum(feat_k, axis=0)), ('rows'...  70.4 us
    gather x18, local copies, waits for them, and re-layouts, add_block(): picked = source_blocks[row_ids]  61.2 us
    reduce_scatter x1, waiting for transfers between devices, per_device(): lax.psum_scatter(partial_rows, 'cols', scatter_dimension=0, tiled=True)  60.9 us
    dot_general x20, matrix products, hi_dot(): return jnp.dot(left, right, precision=lax.Precision.HIGHEST)  42.3 us
  transfers between devices with their start and end apart: 6, of which 4 were waited for; matrix products, arithmetic and copies ran while one was open for 38% of the time, Pallas kernels for 0%

commit v1 on v0

v1 whole, which is shorter than its diff:
```python
import jax
import jax.numpy as jnp
from jax import lax
from jax.experimental import pallas as pl
from jax.experimental.pallas import tpu as pltpu
from jax.sharding import PartitionSpec as P

MESH = pl.DeviceIdType.MESH
F32, BF16 = jnp.float32, jnp.bfloat16
TILE, D, NODE, MAXT = 128, 256, 768, 288
HALF, QUART = NODE // 2, NODE // 4
BLK = NODE // TILE
CH = 256
NN, NT, TN = ((1,), (0,)), ((1,), (1,)), ((0,), (0,))


def dot(a, b, dims=NN):
    return lax.dot_general(
        a, b, (dims, ((), ())), precision=lax.Precision.HIGHEST, preferred_element_type=F32
    )


def feat(v):
    return jnp.where(v > 0, v + 1.0, jnp.exp(jnp.minimum(v, 0.0)))


def slope(v):
    return jnp.where(v > 0, 1.0, jnp.exp(jnp.minimum(v, 0.0)))


def split2(v):
    hi = v.astype(BF16)
    return hi, (v - hi.astype(F32)).astype(BF16)


class Net:
    def __init__(self, ssem, rsem):
        self.ssem, self.rsem, self.n, self.sent = ssem, rsem, 0, []
        self.r, self.c = lax.axis_index("rows"), lax.axis_index("cols")
        self.y, self.x = self.r // 4, self.r % 4
        self.z, self.k = self.c // 2, self.c % 2

    def send(self, src, dst, row=None, col=None):
        i, self.n = self.n, self.n + 1
        copy = pltpu.make_async_remote_copy(
            src_ref=src,
            dst_ref=dst,
            send_sem=self.ssem.at[i],
            recv_sem=self.rsem.at[i],
            device_id=(self.r if row is None else row, self.c if col is None else col),
            device_id_type=MESH,
        )
        copy.start()
        self.sent.append(copy)
        return copy

    def barrier(self):
        sem = pltpu.get_barrier_semaphore()
        there = [(self.r, (self.c + j) % 8) for j in range(1, 8)]
        there += [(self.y * 4 + (self.x + j) % 4, self.c) for j in range(1, 4)]
        there += [((self.y + j) % 4 * 4 + self.x, self.c) for j in range(1, 4)]
        for device in there:
            pl.semaphore_signal(sem, inc=1, device_id=device, device_id_type=MESH)
        pl.semaphore_wait(sem, len(there))

    def finish(self):
        for copy in self.sent:
            copy.wait_send()


def all_reduce(net, part, r1, red1, r2, red2, r3, full1, full):
    r, c, x, y = net.r, net.c, net.x, net.y
    first = []
    for j in range(1, 8):
        to = (c + j) % 8
        first.append(net.send(part.at[pl.ds(to * 4, 4)], r1.at[j - 1], col=to))
    yield
    for copy in first:
        copy.wait_recv()
    total = part[pl.ds(c * 4, 4)]
    for j in range(7):
        total = total + r1[j]
    red1[...] = total
    second = []
    for j in range(1, 4):
        to = (x + j) % 4
        second.append(net.send(red1.at[to], r2.at[j - 1], row=y * 4 + to))
    yield
    for copy in second:
        copy.wait_recv()
    r3[pl.ds(y, 1)] = (red1[pl.ds(x, 1)] + r2[0:1]) + (r2[1:2] + r2[2:3])
    third = [
        net.send(r3.at[y], r3.at[y], row=(y + j) % 4 * 4 + x) for j in range(1, 4)
    ]
    yield
    for copy in third:
        copy.wait_recv()
    full1[pl.ds(x, 1)] = (r3[0:1] + r3[1:2]) + (r3[2:3] + r3[3:4])
    fourth = [
        net.send(full1.at[x], full1.at[x], row=y * 4 + (x + j) % 4) for j in range(1, 4)
    ]
    yield
    for copy in fourth:
        copy.wait_recv()
    full[pl.ds(c * 4, 4)] = full1[...]
    fifth = [
        net.send(full1, full.at[pl.ds(c * 4, 4)], col=(c + j) % 8) for j in range(1, 8)
    ]
    yield
    for copy in fifth:
        copy.wait_recv()


def reduce_scratch(n):
    return [
        pltpu.VMEM((32, n, D), F32),
        pltpu.VMEM((7, 4, n, D), F32),
        pltpu.VMEM((4, n, D), F32),
        pltpu.VMEM((3, n, D), F32),
        pltpu.VMEM((n, D), F32),
        pltpu.VMEM((4, n, D), F32),
        pltpu.VMEM((4, n, D), F32),
        pltpu.VMEM((32, n, D), F32),
    ]


REDUCE_COPIES = 7 + 3 + 3 + 3 + 7


def row_order(net, base):
    if base == 0:
        return net.x, net.y, lambda first, then: then % 4 * 4 + first % 4
    return net.y, net.x, lambda first, then: first % 4 * 4 + then % 4


def gather_half(net, mine, panel, base, done):
    a, b, slot = row_order(net, base)
    all_rows, up, down = pl.ds(base, HALF), pl.ds(base, QUART), pl.ds(base + QUART, QUART)

    def pair(src, at, rows, plus, minus):
        view = panel.at[at, rows]
        source = view if src is None else src.at[rows]
        return net.send(source, view, row=plus), net.send(source, view, row=minus)

    def forward(at, rows, row):
        return net.send(panel.at[at, rows], panel.at[at, rows], row=row)

    own = slot(a, b)
    a_plus, a_minus = slot(a + 1, b), slot(a - 1 + 4, b)
    b_plus, b_minus = slot(a, b + 1), slot(a, b - 1 + 4)
    from_left, from_right = pair(mine, own, all_rows, a_plus, a_minus)
    second = {0: pair(mine, own, all_rows, b_plus, b_minus)}
    yield
    from_left.wait_recv()
    fwd_up = forward(slot(a + 3, b), up, a_plus)
    second[3] = pair(None, slot(a + 3, b), all_rows, b_plus, b_minus)
    from_right.wait_recv()
    fwd_down = forward(slot(a + 1, b), down, a_minus)
    second[1] = pair(None, slot(a + 1, b), all_rows, b_plus, b_minus)
    done(3, 0)
    done(1, 0)
    third = {}

    def pass_on(o):
        left, right = second[o]
        left.wait_recv()
        f_up = forward(slot(a + o, b + 3), up, b_plus)
        right.wait_recv()
        f_down = forward(slot(a + o, b + 1), down, b_minus)
        third[o] = (f_up, f_down)
        done(o, 3)
        done(o, 1)

    yield
    pass_on(0)
    yield
    fwd_up.wait_recv()
    fwd_down.wait_recv()
    second[2] = pair(None, slot(a + 2, b), all_rows, b_plus, b_minus)
    done(2, 0)
    yield
    pass_on(3)
    yield
    pass_on(1)
    yield
    for copy in third[0]:
        copy.wait_recv()
    done(0, 2)
    yield
    pass_on(2)
    yield
    for o in (3, 1, 2):
        for copy in third[o]:
            copy.wait_recv()
        done(o, 2)
        yield


GATHER_COPIES = 2 + 2 + 4 * 4


def gather_cols(net, mine, panel, done):
    z, k = net.z, net.k
    own = net.c
    plus, minus = (z + 1) % 4 * 2 + k, (z + 3) % 4 * 2 + k
    opposite = (z + 2) % 4 * 2 + k
    sibling = z * 2 + 1 - k
    up, down = pl.ds(0, HALF), pl.ds(HALF, HALF)
    left = net.send(mine, panel.at[own], col=plus)
    right = net.send(mine, panel.at[own], col=minus)
    pair = [net.send(mine, panel.at[own], col=sibling)]
    yield
    left.wait_recv()
    f_up = net.send(panel.at[minus, up], panel.at[minus, up], col=plus)
    pair.append(net.send(panel.at[minus], panel.at[minus], col=sibling))
    right.wait_recv()
    f_down = net.send(panel.at[plus, down], panel.at[plus, down], col=minus)
    pair.append(net.send(panel.at[plus], panel.at[plus], col=sibling))
    done(minus)
    done(plus)
    yield
    f_up.wait_recv()
    f_down.wait_recv()
    pair.append(net.send(panel.at[opposite], panel.at[opposite], col=sibling))
    done(opposite)
    yield
    for o, copy in zip((0, 3, 1, 2), pair):
        copy.wait_recv()
        done((z + o) % 4 * 2 + 1 - k)
    yield


COLS_COPIES = 3 + 4 + 1


def drive(*runs):
    runs = list(runs)
    while runs:
        for run in list(runs):
            try:
                next(run)
            except StopIteration:
                runs.remove(run)


def gather_kernel(
    x_ref, c_ref, wq_ref, wk_ref, wv_ref,
    xs_ref, cs_ref, att_ref, gq_ref, key_ref, val_ref, gs_ref, gks_ref,
    q_ref, xp, cp, x_stage, c_stage, stage_sem, ssem, rsem, *reduce_refs,
):
    net = Net(ssem, rsem)
    net.barrier()
    ar1, ar2 = reduce_refs[:8], reduce_refs[8:]
    staged = []

    def split_out(source, stage, out, slot):
        @pl.loop(0, BLK)
        def _(i):
            hi, lo = split2(source[pl.ds(pl.multiple_of(i * TILE, TILE), TILE), :])
            stage[slot, i, 0:TILE, :] = hi
            stage[slot, i, TILE : 2 * TILE, :] = lo

        copy = pltpu.make_async_copy(stage.at[slot], out.at[slot], stage_sem.at[len(staged)])
        copy.start()
        staged.append(copy)

    seen = set()

    def x_done(dx, dy):
        if (dx, dy) in seen:
            slot = (net.y + dy) % 4 * 4 + (net.x + dx) % 4
            split_out(xp.at[slot], x_stage, xs_ref, slot)
        seen.add((dx, dy))

    def cols_done(slot):
        split_out(cp.at[slot], c_stage, cs_ref, slot)

    def attention():
        part, full = ar1[0], ar1[7]
        part2, full2 = ar2[0], ar2[7]

        def first(i, sums):
            state, key_sum = sums
            rows = pl.ds(pl.multiple_of(i * CH, CH), CH)
            x = x_ref[rows, :]
            q_ref[rows, :] = dot(x, wq_ref[...])
            key = dot(x, wk_ref[...])
            val = dot(x, wv_ref[...])
            key_ref[rows, :] = key
            val_ref[rows, :] = val
            feat_k = feat(key)
            return state + dot(feat_k, val, TN), key_sum + jnp.sum(feat_k, axis=0, keepdims=True)

        zero = (jnp.zeros((D, D), F32), jnp.zeros((1, D), F32))
        state, key_sum = lax.fori_loop(0, NODE // CH, first, zero)
        part[:, 0:8, :] = state.reshape(32, 8, D)
        part[:, 8:16, :] = jnp.broadcast_to(key_sum[None], (32, 8, D))
        yield from all_reduce(net, *ar1)
        state_ref, key_row = full, full[0, 8:9, :]
        state = state_ref[:, 0:8, :].reshape(D, D)

        def second(i, sums):
            grad_state, grad_key_sum = sums
            rows = pl.ds(pl.multiple_of(i * CH, CH), CH)
            q = q_ref[rows, :]
            cot = c_ref[rows, :]
            feat_q = feat(q)
            den = jnp.sum(feat_q * key_row, axis=1, keepdims=True)
            att = dot(feat_q, state) / den
            att_ref[rows, :] = att
            scaled = cot / den
            weight_dot = jnp.sum(cot * att, axis=1, keepdims=True) / den
            gq_ref[rows, :] = (dot(scaled, state, NT) - weight_dot * key_row) * slope(q)
            return (
                grad_state + dot(feat_q, scaled, TN),
                grad_key_sum - jnp.sum(feat_q * weight_dot, axis=0, keepdims=True),
            )

        grad_state, grad_key_sum = lax.fori_loop(0, NODE // CH, second, zero)
        part2[:, 0:8, :] = grad_state.reshape(32, 8, D)
        part2[:, 8:16, :] = jnp.broadcast_to(grad_key_sum[None], (32, 8, D))
        yield from all_reduce(net, *ar2)
        gs_ref[...] = full2[:, 0:8, :].reshape(D, D)
        gks_ref[...] = full2[0, 8:16, :]

    def own_blocks():
        yield
        split_out(x_ref, x_stage, xs_ref, net.r)
        split_out(c_ref, c_stage, cs_ref, net.c)

    drive(
        gather_half(net, x_ref, xp, 0, x_done),
        gather_half(net, x_ref, xp, HALF, lambda dy, dx: x_done(dx, dy)),
        gather_cols(net, c_ref, cp, cols_done),
        attention(),
        own_blocks(),
    )
    net.finish()
    for copy in staged:
        copy.wait()


def run_gather(x, cot, wq, wk, wv):
    copies = 2 * GATHER_COPIES + COLS_COPIES + 2 * REDUCE_COPIES
    block = jax.ShapeDtypeStruct((NODE, D), F32)
    vmem, hbm = pl.BlockSpec(memory_space=pltpu.VMEM), pl.BlockSpec(memory_space=pl.ANY)
    return pl.pallas_call(
        gather_kernel,
        out_shape=[
            jax.ShapeDtypeStruct((16, BLK, 2 * TILE, D), BF16),
            jax.ShapeDtypeStruct((8, BLK, 2 * TILE, D), BF16),
            block, block, block, block,
            jax.ShapeDtypeStruct((D, D), F32),
            jax.ShapeDtypeStruct((8, D), F32),
        ],
        in_specs=[vmem] * 5,
        out_specs=[hbm, hbm] + [vmem] * 6,
        scratch_shapes=[
            pltpu.VMEM((NODE, D), F32),
            pltpu.VMEM((16, NODE, D), F32),
            pltpu.VMEM((8, NODE, D), F32),
            pltpu.VMEM((16, BLK, 2 * TILE, D), BF16),
            pltpu.VMEM((8, BLK, 2 * TILE, D), BF16),
            pltpu.SemaphoreType.DMA((24,)),
            pltpu.SemaphoreType.DMA((copies,)),
            pltpu.SemaphoreType.DMA((copies,)),
        ]
        + reduce_scratch(16)
        + reduce_scratch(16),
        compiler_params=pltpu.CompilerParams(
            collective_id=0, has_side_effects=True, vmem_limit_bytes=60 * 2**20
        ),
        name="gather",
    )(x, cot, wq, wk, wv)


CHUNK = 16
SLOTS = 3
GROUP = 4


def tile_kernel(
    rows_ref, cols_ref, count_ref, tiles_ref, xs_ref, cs_ref,
    f_ref, t_ref,
    xs, cs, f, t, buf, sem, tile_sem,
):
    count = count_ref[0]
    chunks = (count + CHUNK - 1) // CHUNK
    load_c = pltpu.make_async_copy(cs_ref, cs, sem.at[0])
    load_x = pltpu.make_async_copy(xs_ref, xs, sem.at[1])

    def fetch(chunk, slot):
        return pltpu.make_async_copy(
            tiles_ref.at[pl.ds(chunk * CHUNK, CHUNK)], buf.at[slot], tile_sem.at[slot]
        )

    def sweep(body):
        for i in range(SLOTS - 1):
            @pl.when(i < chunks)
            def _(i=i):
                fetch(i, i).start()

        @pl.loop(0, chunks)
        def _(chunk):
            slot = chunk % SLOTS

            @pl.when(chunk + SLOTS - 1 < chunks)
            def _():
                fetch(chunk + SLOTS - 1, (chunk + SLOTS - 1) % SLOTS).start()

            fetch(chunk, slot).wait()

            @pl.loop(0, CHUNK // GROUP)
            def _(group):
                first = group * GROUP
                for i in range(GROUP):
                    at = chunk * CHUNK + first + i
                    tile = buf[slot, first + i]
                    body(jnp.where(at < count, tile, 0.0), rows_ref[at], cols_ref[at])

    def product(tile, panel):
        hi, lo = split2(tile)
        left = jnp.concatenate(
            [jnp.concatenate([hi, hi], axis=1), jnp.concatenate([lo, lo], axis=1)], axis=0
        )
        both = jnp.dot(left, panel, preferred_element_type=F32)
        return both[0:TILE] + both[TILE : 2 * TILE]

    def backward(tile, row, col):
        t[col] += product(tile.T, cs[row])

    def forward(tile, row, col):
        f[row] += product(tile, xs[col])

    load_c.start()
    load_x.start()
    t[...] = jnp.zeros_like(t)
    f[...] = jnp.zeros_like(f)
    load_c.wait()
    sweep(backward)
    store_t = pltpu.make_async_copy(t, t_ref, sem.at[2])
    store_t.start()
    load_x.wait()
    sweep(forward)
    store_f = pltpu.make_async_copy(f, f_ref, sem.at[3])
    store_f.start()
    store_t.wait()
    store_f.wait()


def run_tiles(tile_rows, tile_cols, tile_count, tiles, xs, cs):
    hbm, smem = pl.BlockSpec(memory_space=pl.ANY), pl.BlockSpec(memory_space=pltpu.SMEM)
    return pl.pallas_call(
        tile_kernel,
        out_shape=[
            jax.ShapeDtypeStruct((8 * BLK, TILE, D), F32),
            jax.ShapeDtypeStruct((16 * BLK, TILE, D), F32),
        ],
        in_specs=[smem] * 3 + [hbm] * 3,
        out_specs=[hbm] * 2,
        scratch_shapes=[
            pltpu.VMEM((16 * BLK, 2 * TILE, D), BF16),
            pltpu.VMEM((8 * BLK, 2 * TILE, D), BF16),
            pltpu.VMEM((8 * BLK, TILE, D), F32),
            pltpu.VMEM((16 * BLK, TILE, D), F32),
            pltpu.VMEM((SLOTS, CHUNK, TILE, TILE), F32),
            pltpu.SemaphoreType.DMA((4,)),
            pltpu.SemaphoreType.DMA((SLOTS,)),
        ],
        compiler_params=pltpu.CompilerParams(vmem_limit_bytes=60 * 2**20),
        name="tiles",
    )(
        tile_rows, tile_cols, tile_count, tiles,
        xs.reshape(16 * BLK, 2 * TILE, D), cs.reshape(8 * BLK, 2 * TILE, D),
    )


def scatter_half(net, t_hbm, t, base, leaf, main, leaf2, main2, ready):
    s, b, slot = row_order(net, base)
    up, down, both = pl.ds(base, QUART), pl.ds(base + QUART, QUART), pl.ds(base, HALF)
    order = (2, 1, 3, 0)
    b_plus, b_minus = slot(s, b + 1), slot(s, b + 3)
    leaves, mains = [], []
    for i, o in enumerate(order):
        at = slot(s + o, b + 2)
        leaves.append(
            (
                net.send(t_hbm.at[at, up], leaf.at[i, 0], row=b_plus),
                net.send(t_hbm.at[at, down], leaf.at[i, 1], row=b_minus),
            )
        )
    yield
    ready()
    for i, o in enumerate(order):
        for copy in leaves[i]:
            copy.wait_recv()
        plus, minus = slot(s + o, b + 1), slot(s + o, b + 3)
        t[plus, up] += leaf[i, 0]
        t[minus, down] += leaf[i, 1]
        mains.append(
            (
                net.send(t.at[plus, both], main.at[i, 0], row=b_plus),
                net.send(t.at[minus, both], main.at[i, 1], row=b_minus),
            )
        )
        yield
    s_plus, s_minus = slot(s + 1, b), slot(s + 3, b)
    for i, o in enumerate(order):
        for copy in mains[i]:
            copy.wait_recv()
        at = slot(s + o, b)
        t[at, both] += main[i, 0] + main[i, 1]
        if o == 2:
            leaves2 = (
                net.send(t.at[at, up], leaf2.at[0], row=s_plus),
                net.send(t.at[at, down], leaf2.at[1], row=s_minus),
            )
        if o == 3:
            for copy in leaves2:
                copy.wait_recv()
            t[s_plus, up] += leaf2[0]
            t[s_minus, down] += leaf2[1]
            mains2 = (
                net.send(t.at[s_plus, both], main2.at[0], row=s_plus),
                net.send(t.at[s_minus, both], main2.at[1], row=s_minus),
            )
        yield
    for copy in mains2:
        copy.wait_recv()
    t[slot(s, b), both] += main2[0] + main2[1]


SCATTER_COPIES = GATHER_COPIES


def scatter_cols(net, f_hbm, f, pair, leaf, main, ready):
    z, k = net.z, net.k
    up, down = pl.ds(0, HALF), pl.ds(HALF, HALF)
    order = (2, 1, 3, 0)
    copies = [
        net.send(f_hbm.at[(z + o) % 4 * 2 + 1 - k], pair.at[i], col=z * 2 + 1 - k)
        for i, o in enumerate(order)
    ]
    yield
    ready()
    plus, minus = (z + 1) % 4 * 2 + k, (z + 3) % 4 * 2 + k
    for i, o in enumerate(order):
        copies[i].wait_recv()
        at = (z + o) % 4 * 2 + k
        f[at] += pair[i]
        if o == 2:
            leaves = (
                net.send(f.at[at, up], leaf.at[0], col=plus),
                net.send(f.at[at, down], leaf.at[1], col=minus),
            )
            yield
    yield
    for copy in leaves:
        copy.wait_recv()
    f[plus, up] += leaf[0]
    f[minus, down] += leaf[1]
    mains = (
        net.send(f.at[plus], main.at[0], col=plus),
        net.send(f.at[minus], main.at[1], col=minus),
    )
    yield
    for copy in mains:
        copy.wait_recv()
    f[net.c] += main[0] + main[1]


SCATTER_COLS_COPIES = 4 + 2 + 2


def scatter_kernel(
    x_ref, c_ref, wq_ref, wk_ref, wv_ref, wg_ref,
    att_ref, gq_ref, key_ref, val_ref, gs_ref, gks_ref, f_hbm, t_hbm,
    out_ref, gx_ref, dq_ref, dk_ref, dv_ref, dg_ref,
    f, t, leaf, main, leaf2, main2, pair, zleaf, zmain, load_sem, ssem, rsem, *reduce_refs,
):
    net = Net(ssem, rsem)
    load_t = pltpu.make_async_copy(t_hbm, t, load_sem.at[0])
    load_f = pltpu.make_async_copy(f_hbm, f, load_sem.at[1])
    load_t.start()
    load_f.start()
    net.barrier()
    ar1, ar2 = reduce_refs[:8], reduce_refs[8:]

    def ready(copy):
        pending = [copy]

        def once():
            if pending:
                pending.pop().wait()

        return once

    def attention():
        part, full = ar1[0], ar1[7]
        zero = jnp.zeros((D, D), F32)

        dq_ref[...] = zero
        dk_ref[...] = zero
        dv_ref[...] = zero

        @pl.loop(0, NODE // CH)
        def _(i):
            rows = pl.ds(pl.multiple_of(i * CH, CH), CH)
            x = x_ref[rows, :]
            key = key_ref[rows, :]
            gq = gq_ref[rows, :]
            gk = (dot(val_ref[rows, :], gs_ref[...], NT) + gks_ref[0:1, :]) * slope(key)
            gv = dot(feat(key), gs_ref[...])
            gx = dot(gq, wq_ref[...], NT) + dot(gk, wk_ref[...], NT)
            gx_ref[rows, :] = gx + dot(gv, wv_ref[...], NT)
            dq_ref[...] += dot(x, gq, TN)
            dk_ref[...] += dot(x, gk, TN)
            dv_ref[...] += dot(x, gv, TN)

        for i, grad in enumerate((dq_ref, dk_ref, dv_ref)):
            part[:, 8 * i : 8 * i + 8, :] = grad[...].reshape(32, 8, D)
        yield from all_reduce(net, *ar1)
        for i, grad in enumerate((dq_ref, dk_ref, dv_ref)):
            grad[...] = full[:, 8 * i : 8 * i + 8, :].reshape(D, D)

    def graph():
        part, full = ar2[0], ar2[7]
        yield from scatter_cols(net, f_hbm, f, pair, zleaf, zmain, ready(load_f))
        dg_ref[...] = jnp.zeros((D, D), F32)

        @pl.loop(0, NODE // CH)
        def _(i):
            rows = pl.ds(pl.multiple_of(i * CH, CH), CH)
            mixed = f[net.c, rows, :]
            out_ref[rows, :] = att_ref[rows, :] + dot(mixed, wg_ref[...])
            dg_ref[...] += dot(mixed, c_ref[rows, :], TN)

        part[...] = dg_ref[...].reshape(32, 8, D)
        yield from all_reduce(net, *ar2)
        dg_ref[...] = full[...].reshape(D, D)

    once_t = ready(load_t)
    drive(
        scatter_half(net, t_hbm, t, 0, leaf.at[0], main.at[0], leaf2.at[0], main2.at[0], once_t),
        scatter_half(net, t_hbm, t, HALF, leaf.at[1], main.at[1], leaf2.at[1], main2.at[1], once_t),
        graph(),
        attention(),
    )

    @pl.loop(0, NODE // CH)
    def _(i):
        rows = pl.ds(pl.multiple_of(i * CH, CH), CH)
        gx_ref[rows, :] += dot(t[net.r, rows, :], wg_ref[...], NT)

    net.finish()


def run_scatter(x, cot, wq, wk, wv, wg, att, gq, key, val, gs, gks, f, t):
    copies = 2 * SCATTER_COPIES + SCATTER_COLS_COPIES + 2 * REDUCE_COPIES
    block, weight = jax.ShapeDtypeStruct((NODE, D), F32), jax.ShapeDtypeStruct((D, D), F32)
    vmem, hbm = pl.BlockSpec(memory_space=pltpu.VMEM), pl.BlockSpec(memory_space=pl.ANY)
    return pl.pallas_call(
        scatter_kernel,
        out_shape=[block, block, weight, weight, weight, weight],
        in_specs=[vmem] * 12 + [hbm] * 2,
        out_specs=[vmem] * 6,
        scratch_shapes=[
            pltpu.VMEM((8, NODE, D), F32),
            pltpu.VMEM((16, NODE, D), F32),
            pltpu.VMEM((2, 4, 2, QUART, D), F32),
            pltpu.VMEM((2, 4, 2, HALF, D), F32),
            pltpu.VMEM((2, 2, QUART, D), F32),
            pltpu.VMEM((2, 2, HALF, D), F32),
            pltpu.VMEM((4, NODE, D), F32),
            pltpu.VMEM((2, HALF, D), F32),
            pltpu.VMEM((2, NODE, D), F32),
            pltpu.SemaphoreType.DMA((2,)),
            pltpu.SemaphoreType.DMA((copies,)),
            pltpu.SemaphoreType.DMA((copies,)),
        ]
        + reduce_scratch(24)
        + reduce_scratch(8),
        compiler_params=pltpu.CompilerParams(
            collective_id=1, has_side_effects=True, vmem_limit_bytes=60 * 2**20
        ),
        name="scatter",
    )(x, cot, wq, wk, wv, wg, att, gq, key, val, gs, gks, f, t)


def per_device(x, cot, wq, wk, wv, wg, tiles, tile_rows, tile_cols, tile_count):
    xs, cs, att, gq, key, val, gs, gks = run_gather(x, cot, wq, wk, wv)
    f, t = run_tiles(tile_rows, tile_cols, tile_count, tiles, xs, cs)
    f, t = f.reshape(8, NODE, D), t.reshape(16, NODE, D)
    return tuple(run_scatter(x, cot, wq, wk, wv, wg, att, gq, key, val, gs, gks, f, t))


def solution(mesh):
    nodes = P(("rows", "cols"), None)
    slots = P(("rows", "cols"))
    return jax.shard_map(
        per_device,
        mesh=mesh,
        in_specs=(nodes, nodes, P(), P(), P(), P(), P(("rows", "cols"), None, None), slots, slots, slots),
        out_specs=(nodes, nodes, P(), P(), P(), P()),
        check_vma=False,
    )
```

time: 1150 us -> 267 us (0.23)
  blocking collectives: 454 us -> 0 us
  Pallas kernels: 0 us -> 254 us
  waiting for transfers between devices: 217 us -> 0 us
  local copies, waits for them, and re-layouts: 185 us -> 10.8 us
  other arithmetic: 147 us -> 0 us
  matrix products: 118 us -> 0 us
  between operations: 16.1 us -> 1.31 us
    psum x2 -> x0, blocking collectives: 454 us -> none  [the longest x1 384 us: per_device(): lax.psum((hi_dot(feat_q.T, scaled), -hi_dot(weight_dot, feat_q)), ('rows'...]
    pallas_call x0 -> x3, Pallas kernels: none -> 254 us  [the longest x1 114 us: run_scatter(): pl.pallas_call(scatter_kernel, out_shape=[block, block, weight, weight, w...]
    gather x36 -> x0, local copies, waits for them, and re-layouts: 155 us -> none  [the longest x18 94.1 us: add_block(): picked = source_blocks[col_ids]]
    psum x2 -> x0, waiting for transfers between devices: 143 us -> none  [the longest x1 143 us: per_device(): lax.psum((local_query, local_key, local_value), ('rows', 'cols'))]
    scatter-add x36 -> x0, other arithmetic: 120 us -> none  [add_block(): return running.at[placing_ids].add(product * alive_mask[:, None, None])]
    dot_general x56 -> x0, matrix products: 118 us -> none  [the longest x20 42.3 us: hi_dot(): return jnp.dot(left, right, precision=lax.Precision.HIGHEST)]
    reduce_scatter x2 -> x0, waiting for transfers between devices: 65 us -> none  [the longest x1 60.9 us: per_device(): lax.psum_scatter(partial_rows, 'cols', scatter_dimension=0, tiled=True)]
    convert_element_type x36 -> x0, other arithmetic: 23.4 us -> none  [add_block(): alive_mask = (first_slot + slot_ids < tile_total).astype(jnp.float32)]
  transfers between devices with their start and end apart: 6 -> 0, of which waited for: 4 -> 0; matrix products, arithmetic and copies ran while one was open for 38% -> 0% of each run, Pallas kernels for 0% -> 0%
where the time goes in v1:
time: 267 us
  Pallas kernels  254 us (95%)
  local copies, waits for them, and re-layouts  10.8 us (4%)
    pallas_call x1, Pallas kernels, run_scatter(): pl.pallas_call(scatter_kernel, out_shape=[block, block, weight, weight, w...  114 us
    pallas_call x1, Pallas kernels, run_gather(): pl.pallas_call(gather_kernel, out_shape=[jax.ShapeDtypeStruct((16, BLK, 2...  104 us
    pallas_call x1, Pallas kernels, run_tiles(): pl.pallas_call(tile_kernel, out_shape=[jax.ShapeDtypeStruct((8 * BLK, TIL...  37 us
    unnamed x6, local copies, waits for them, and re-layouts  10.8 us

profile of v1, /device:TPU:1, one launch (start us, length us, event | category | flops | bytes accessed | tf_op | source)
XLA Modules:
  0.0 266.6 jit_solution(5314655005374440290)
XLA Ops:
  1.3 103.6 %gather.1 = (bf16[16,6,256,256]{3,2,1,0:T(8,128)(2,1)}, bf16[8,6,256,256]{3,2,1,0:T(8,128)(2,1)}, f32[768,256]{1,0:T(8,128)}, f32[768,256]{1,0:T(8,128)}, f32[76...) custom-call(f32[768,256]{1,0:T(8,128)} %x_ref.3, f32[768,256]{1,0:T(8,128)} %c_ref.3, ...), custom_call_target="tpu_custom_call" | custom-call | tf_op jit(solution)/shard_map/gather/pallas_call | solution.py:347
  104.9 37.0 %tiles.1 = (f32[48,128,256]{2,1,0:T(8,128)}, f32[96,128,256]{2,1,0:T(8,128)}) custom-call(s32[288]{0:T(512)} %rows_ref.1, s32[288]{0:T(512)} %cols_ref.1, s32[1]{0:T(128)S(6)} %copy.22.count_ref, f32[288,128,128]{2,1,0:T(8,128)} %tiles_ref.1, bf16[96,256,256]{2,1,0:T(8,128)(2,1)} %bitcast.5, bf16[48,256,256]{2,1,0:T(8,128)(2,1)} %bitcast.7), custom_call_target="tpu_custom_call" | custom-call | tf_op jit(solution)/shard_map/tiles/pallas_call | solution.py:453
  142.0 113.8 %scatter.1 = (f32[768,256]{1,0:T(8,128)}, f32[768,256]{1,0:T(8,128)}, f32[256,256]{1,0:T(8,128)}, f32[256,256]{1,0:T(8,128)}, f32[256,256]{1,0:T(8,128)}, /*index=5*/f32[256,256]{1,0:T(8,128)}) custom-call(f32[768,256]{1,0:T(8,128)} %x_ref.3, f32[768,256]{1,0:T(8,128)} %c_ref.3, f32[256,256]{1,0:T(8,128)} %wq_ref.3, f32[256,256]{1,0:T(8,128)} %wk_ref.3, ...), custom_call_target="tpu_custom_call" | custom-call | tf_op jit(solution)/shard_map/scatter/pallas_call | solution.py:662
  255.8 2.1 copy.23
  257.8 2.1 copy.24
  259.9 1.7 copy.25
  261.6 1.7 copy.26
  263.2 1.7 copy.27
  264.9 1.7 copy.28

commit v2 on v1

--- a/solution.py
+++ b/solution.py
@@ -10,14 +10,17 @@
 TILE, D, NODE, MAXT = 128, 256, 768, 288
 HALF, QUART = NODE // 2, NODE // 4
 BLK = NODE // TILE
-CH = 256
+CH = 384
 NN, NT, TN = ((1,), (0,)), ((1,), (1,)), ((0,), (0,))
 
 
 def dot(a, b, dims=NN):
-    return lax.dot_general(
-        a, b, (dims, ((), ())), precision=lax.Precision.HIGHEST, preferred_element_type=F32
-    )
+    (a_hi, a_lo), (b_hi, b_lo) = split2(a), split2(b)
+
+    def one(p, q):
+        return lax.dot_general(p, q, (dims, ((), ())), preferred_element_type=F32)
+
+    return one(a_hi, b_hi) + (one(a_hi, b_lo) + one(a_lo, b_hi))
 
 
 def feat(v):
@@ -68,63 +71,57 @@
             copy.wait_send()
 
 
-def all_reduce(net, part, r1, red1, r2, red2, r3, full1, full):
-    r, c, x, y = net.r, net.c, net.x, net.y
-    first = []
-    for j in range(1, 8):
-        to = (c + j) % 8
-        first.append(net.send(part.at[pl.ds(to * 4, 4)], r1.at[j - 1], col=to))
+def all_reduce(net, part, key, r1, kbuf, r2, r3, full):
+    c, x, y = net.c, net.x, net.y
+    n = part.shape[1]
+    first = [net.send(part.at[(c + j) % 8], r1.at[j - 1], col=(c + j) % 8) for j in range(1, 8)]
+    if key is not None:
+        first += [net.send(key, kbuf.at[j - 1], col=(c + j) % 8) for j in range(1, 8)]
     yield
     for copy in first:
         copy.wait_recv()
-    total = part[pl.ds(c * 4, 4)]
+    total = part[c]
     for j in range(7):
         total = total + r1[j]
-    red1[...] = total
-    second = []
-    for j in range(1, 4):
-        to = (x + j) % 4
-        second.append(net.send(red1.at[to], r2.at[j - 1], row=y * 4 + to))
+    r2[x, 0:n] = total
+    if key is not None:
+        total = key[...]
+        for j in range(7):
+            total = total + kbuf[j]
+        r2[x, n:] = total
+    second = [net.send(r2.at[x], r2.at[x], row=y * 4 + (x + j) % 4) for j in range(1, 4)]
     yield
     for copy in second:
         copy.wait_recv()
-    r3[pl.ds(y, 1)] = (red1[pl.ds(x, 1)] + r2[0:1]) + (r2[1:2] + r2[2:3])
-    third = [
-        net.send(r3.at[y], r3.at[y], row=(y + j) % 4 * 4 + x) for j in range(1, 4)
+    r3[y] = (r2[0] + r2[1]) + (r2[2] + r2[3])
+    third = [net.send(r3.at[y], r3.at[y], row=(y + j) % 4 * 4 + x) for j in range(1, 4)]
+    yield
+    for copy in third:
+        copy.wait_recv()
+    full[c] = (r3[0, 0:n] + r3[1, 0:n]) + (r3[2, 0:n] + r3[3, 0:n])
+    fourth = [net.send(full.at[c], full.at[c], col=(c + j) % 8) for j in range(1, 8)]
+    yield
+    for copy in fourth:
+        copy.wait_recv()
+
+
+def key_total(r3, n):
+    return (r3[0, n:] + r3[1, n:]) + (r3[2, n:] + r3[3, n:])
+
+
+def reduce_scratch(n, extra):
+    return [
+        pltpu.VMEM((8, n, D), F32),
+        pltpu.VMEM((8, D), F32),
+        pltpu.VMEM((7, n, D), F32),
+        pltpu.VMEM((7, 8, D), F32),
+        pltpu.VMEM((4, n + extra, D), F32),
+        pltpu.VMEM((4, n + extra, D), F32),
+        pltpu.VMEM((8, n, D), F32),
     ]
-    yield
-    for copy in third:
-        copy.wait_recv()
-    full1[pl.ds(x, 1)] = (r3[0:1] + r3[1:2]) + (r3[2:3] + r3[3:4])
-    fourth = [
-        net.send(full1.at[x], full1.at[x], row=y * 4 + (x + j) % 4) for j in range(1, 4)
-    ]
-    yield
-    for copy in fourth:
-        copy.wait_recv()
-    full[pl.ds(c * 4, 4)] = full1[...]
-    fifth = [
-        net.send(full1, full.at[pl.ds(c * 4, 4)], col=(c + j) % 8) for j in range(1, 8)
-    ]
-    yield
-    for copy in fifth:
-        copy.wait_recv()
-
-
-def reduce_scratch(n):
-    return [
-        pltpu.VMEM((32, n, D), F32),
-        pltpu.VMEM((7, 4, n, D), F32),
-        pltpu.VMEM((4, n, D), F32),
-        pltpu.VMEM((3, n, D), F32),
-        pltpu.VMEM((n, D), F32),
-        pltpu.VMEM((4, n, D), F32),
-        pltpu.VMEM((4, n, D), F32),
-        pltpu.VMEM((32, n, D), F32),
-    ]
-
-
-REDUCE_COPIES = 7 + 3 + 3 + 3 + 7
+
+
+REDUCE_COPIES = 7 + 7 + 3 + 3 + 7
 
 
 def row_order(net, base):
@@ -149,6 +146,7 @@
     a_plus, a_minus = slot(a + 1, b), slot(a - 1 + 4, b)
     b_plus, b_minus = slot(a, b + 1), slot(a, b - 1 + 4)
     from_left, from_right = pair(mine, own, all_rows, a_plus, a_minus)
+    yield
     second = {0: pair(mine, own, all_rows, b_plus, b_minus)}
     yield
     from_left.wait_recv()
@@ -156,6 +154,7 @@
     second[3] = pair(None, slot(a + 3, b), all_rows, b_plus, b_minus)
     from_right.wait_recv()
     fwd_down = forward(slot(a + 1, b), down, a_minus)
+    yield
     second[1] = pair(None, slot(a + 1, b), all_rows, b_plus, b_minus)
     done(3, 0)
     done(1, 0)
@@ -233,14 +232,22 @@
 COLS_COPIES = 3 + 4 + 1
 
 
-def drive(*runs):
-    runs = list(runs)
+def drive(order, **runs):
+    def step(name):
+        try:
+            next(runs[name])
+        except StopIteration:
+            del runs[name]
+
+    for name in order:
+        if name in runs:
+            step(name)
     while runs:
-        for run in list(runs):
-            try:
-                next(run)
-            except StopIteration:
-                runs.remove(run)
+        for name in list(runs):
+            step(name)
+
+
+GATHER_ORDER = "abtctabotabtabtctababctababtcabtab"
 
 
 def gather_kernel(
@@ -250,7 +257,7 @@
 ):
     net = Net(ssem, rsem)
     net.barrier()
-    ar1, ar2 = reduce_refs[:8], reduce_refs[8:]
+    ar1, ar2 = reduce_refs[:7], reduce_refs[7:]
     staged = []
 
     def split_out(source, stage, out, slot):
@@ -276,9 +283,6 @@
         split_out(cp.at[slot], c_stage, cs_ref, slot)
 
     def attention():
-        part, full = ar1[0], ar1[7]
-        part2, full2 = ar2[0], ar2[7]
-
         def first(i, sums):
             state, key_sum = sums
             rows = pl.ds(pl.multiple_of(i * CH, CH), CH)
@@ -293,11 +297,11 @@
 
         zero = (jnp.zeros((D, D), F32), jnp.zeros((1, D), F32))
         state, key_sum = lax.fori_loop(0, NODE // CH, first, zero)
-        part[:, 0:8, :] = state.reshape(32, 8, D)
-        part[:, 8:16, :] = jnp.broadcast_to(key_sum[None], (32, 8, D))
+        ar1[0][...] = state.reshape(8, 32, D)
+        ar1[1][...] = jnp.broadcast_to(key_sum, (8, D))
         yield from all_reduce(net, *ar1)
-        state_ref, key_row = full, full[0, 8:9, :]
-        state = state_ref[:, 0:8, :].reshape(D, D)
+        state = ar1[6][...].reshape(D, D)
+        key_row = key_total(ar1[5], 32)[0:1]
 
         def second(i, sums):
             grad_state, grad_key_sum = sums
@@ -317,11 +321,11 @@
             )
 
         grad_state, grad_key_sum = lax.fori_loop(0, NODE // CH, second, zero)
-        part2[:, 0:8, :] = grad_state.reshape(32, 8, D)
-        part2[:, 8:16, :] = jnp.broadcast_to(grad_key_sum[None], (32, 8, D))
+        ar2[0][...] = grad_state.reshape(8, 32, D)
+        ar2[1][...] = jnp.broadcast_to(grad_key_sum, (8, D))
         yield from all_reduce(net, *ar2)
-        gs_ref[...] = full2[:, 0:8, :].reshape(D, D)
-        gks_ref[...] = full2[0, 8:16, :]
+        gs_ref[...] = ar2[6][...].reshape(D, D)
+        gks_ref[...] = key_total(ar2[5], 32)
 
     def own_blocks():
         yield
@@ -329,11 +333,12 @@
         split_out(c_ref, c_stage, cs_ref, net.c)
 
     drive(
-        gather_half(net, x_ref, xp, 0, x_done),
-        gather_half(net, x_ref, xp, HALF, lambda dy, dx: x_done(dx, dy)),
-        gather_cols(net, c_ref, cp, cols_done),
-        attention(),
-        own_blocks(),
+        GATHER_ORDER,
+        a=gather_half(net, x_ref, xp, 0, x_done),
+        b=gather_half(net, x_ref, xp, HALF, lambda dy, dx: x_done(dx, dy)),
+        c=gather_cols(net, c_ref, cp, cols_done),
+        t=attention(),
+        o=own_blocks(),
     )
     net.finish()
     for copy in staged:
@@ -365,8 +370,8 @@
             pltpu.SemaphoreType.DMA((copies,)),
             pltpu.SemaphoreType.DMA((copies,)),
         ]
-        + reduce_scratch(16)
-        + reduce_scratch(16),
+        + reduce_scratch(32, 8)
+        + reduce_scratch(32, 8),
         compiler_params=pltpu.CompilerParams(
             collective_id=0, has_side_effects=True, vmem_limit_bytes=60 * 2**20
         ),
@@ -376,7 +381,7 @@
 
 CHUNK = 16
 SLOTS = 3
-GROUP = 4
+GROUP = 16
 
 
 def tile_kernel(
@@ -420,11 +425,8 @@
 
     def product(tile, panel):
         hi, lo = split2(tile)
-        left = jnp.concatenate(
-            [jnp.concatenate([hi, hi], axis=1), jnp.concatenate([lo, lo], axis=1)], axis=0
-        )
-        both = jnp.dot(left, panel, preferred_element_type=F32)
-        return both[0:TILE] + both[TILE : 2 * TILE]
+        whole = jnp.dot(jnp.concatenate([hi, hi], axis=1), panel, preferred_element_type=F32)
+        return whole + jnp.dot(lo, panel[0:TILE], preferred_element_type=F32)
 
     def backward(tile, row, col):
         t[col] += product(tile.T, cs[row])
@@ -475,7 +477,7 @@
     )
 
 
-def scatter_half(net, t_hbm, t, base, leaf, main, leaf2, main2, ready):
+def scatter_half(net, t_hbm, t, base, leaf, main, leaf2, main2, own_ref, ready):
     s, b, slot = row_order(net, base)
     up, down, both = pl.ds(base, QUART), pl.ds(base + QUART, QUART), pl.ds(base, HALF)
     order = (2, 1, 3, 0)
@@ -489,45 +491,61 @@
                 net.send(t_hbm.at[at, down], leaf.at[i, 1], row=b_minus),
             )
         )
-    yield
-    ready()
-    for i, o in enumerate(order):
+        if i == 1:
+            yield
+    s_plus, s_minus = slot(s + 1, b), slot(s + 3, b)
+
+    def main_sends(i):
         for copy in leaves[i]:
             copy.wait_recv()
-        plus, minus = slot(s + o, b + 1), slot(s + o, b + 3)
+        plus, minus = slot(s + order[i], b + 1), slot(s + order[i], b + 3)
         t[plus, up] += leaf[i, 0]
         t[minus, down] += leaf[i, 1]
-        mains.append(
-            (
-                net.send(t.at[plus, both], main.at[i, 0], row=b_plus),
-                net.send(t.at[minus, both], main.at[i, 1], row=b_minus),
-            )
+        return (
+            net.send(t.at[plus, both], main.at[i, 0], row=b_plus),
+            net.send(t.at[minus, both], main.at[i, 1], row=b_minus),
         )
-        yield
-    s_plus, s_minus = slot(s + 1, b), slot(s + 3, b)
-    for i, o in enumerate(order):
+
+    def collect(i):
         for copy in mains[i]:
             copy.wait_recv()
-        at = slot(s + o, b)
+        at = slot(s + order[i], b)
         t[at, both] += main[i, 0] + main[i, 1]
-        if o == 2:
-            leaves2 = (
-                net.send(t.at[at, up], leaf2.at[0], row=s_plus),
-                net.send(t.at[at, down], leaf2.at[1], row=s_minus),
-            )
-        if o == 3:
-            for copy in leaves2:
-                copy.wait_recv()
-            t[s_plus, up] += leaf2[0]
-            t[s_minus, down] += leaf2[1]
-            mains2 = (
-                net.send(t.at[s_plus, both], main2.at[0], row=s_plus),
-                net.send(t.at[s_minus, both], main2.at[1], row=s_minus),
-            )
-        yield
+        return at
+
+    yield
+    ready()
+    mains.append(main_sends(0))
+    yield
+    mains.append(main_sends(1))
+    yield
+    mains.append(main_sends(2))
+    yield
+    at = collect(0)
+    leaves2 = (
+        net.send(t.at[at, up], leaf2.at[0], row=s_plus),
+        net.send(t.at[at, down], leaf2.at[1], row=s_minus),
+    )
+    yield
+    mains.append(main_sends(3))
+    yield
+    collect(1)
+    yield
+    collect(2)
+    for copy in leaves2:
+        copy.wait_recv()
+    t[s_plus, up] += leaf2[0]
+    t[s_minus, down] += leaf2[1]
+    mains2 = (
+        net.send(t.at[s_plus, both], main2.at[0], row=s_plus),
+        net.send(t.at[s_minus, both], main2.at[1], row=s_minus),
+    )
+    yield
+    collect(3)
+    yield
     for copy in mains2:
         copy.wait_recv()
-    t[slot(s, b), both] += main2[0] + main2[1]
+    own_ref[both, :] = t[slot(s, b), both] + (main2[0] + main2[1])
 
 
 SCATTER_COPIES = GATHER_COPIES
@@ -572,10 +590,13 @@
 SCATTER_COLS_COPIES = 4 + 2 + 2
 
 
+SCATTER_ORDER = "abgtabttgabgtabgtababtabgabtgabgabgabg"
+
+
 def scatter_kernel(
     x_ref, c_ref, wq_ref, wk_ref, wv_ref, wg_ref,
     att_ref, gq_ref, key_ref, val_ref, gs_ref, gks_ref, f_hbm, t_hbm,
-    out_ref, gx_ref, dq_ref, dk_ref, dv_ref, dg_ref,
+    own_ref, out_ref, gx_ref, dq_ref, dk_ref, dv_ref, dg_ref,
     f, t, leaf, main, leaf2, main2, pair, zleaf, zmain, load_sem, ssem, rsem, *reduce_refs,
 ):
     net = Net(ssem, rsem)
@@ -584,7 +605,7 @@
     load_t.start()
     load_f.start()
     net.barrier()
-    ar1, ar2 = reduce_refs[:8], reduce_refs[8:]
+    ar1, ar2 = reduce_refs[:7], reduce_refs[7:]
 
     def ready(copy):
         pending = [copy]
@@ -596,16 +617,8 @@
         return once
 
     def attention():
-        part, full = ar1[0], ar1[7]
-        zero = jnp.zeros((D, D), F32)
-
-        dq_ref[...] = zero
-        dk_ref[...] = zero
-        dv_ref[...] = zero
-
-        @pl.loop(0, NODE // CH)
-        def _(i):
-            rows = pl.ds(pl.multiple_of(i * CH, CH), CH)
+        for i in range(NODE // CH):
+            rows = pl.ds(i * CH, CH)
             x = x_ref[rows, :]
             key = key_ref[rows, :]
             gq = gq_ref[rows, :]
@@ -613,18 +626,16 @@
             gv = dot(feat(key), gs_ref[...])
             gx = dot(gq, wq_ref[...], NT) + dot(gk, wk_ref[...], NT)
             gx_ref[rows, :] = gx + dot(gv, wv_ref[...], NT)
-            dq_ref[...] += dot(x, gq, TN)
-            dk_ref[...] += dot(x, gk, TN)
-            dv_ref[...] += dot(x, gv, TN)
-
-        for i, grad in enumerate((dq_ref, dk_ref, dv_ref)):
-            part[:, 8 * i : 8 * i + 8, :] = grad[...].reshape(32, 8, D)
-        yield from all_reduce(net, *ar1)
-        for i, grad in enumerate((dq_ref, dk_ref, dv_ref)):
-            grad[...] = full[:, 8 * i : 8 * i + 8, :].reshape(D, D)
+            for j, grad in enumerate((gq, gk, gv)):
+                product = dot(x, grad, TN).reshape(8, 32, D)
+                at = pl.ds(32 * j, 32)
+                ar1[0][:, at, :] = product if i == 0 else ar1[0][:, at, :] + product
+            yield
+        yield from all_reduce(net, ar1[0], None, *ar1[2:])
+        for j, grad in enumerate((dq_ref, dk_ref, dv_ref)):
+            grad[...] = ar1[6][:, pl.ds(32 * j, 32), :].reshape(D, D)
 
     def graph():
-        part, full = ar2[0], ar2[7]
         yield from scatter_cols(net, f_hbm, f, pair, zleaf, zmain, ready(load_f))
         dg_ref[...] = jnp.zeros((D, D), F32)
 
@@ -635,23 +646,18 @@
             out_ref[rows, :] = att_ref[rows, :] + dot(mixed, wg_ref[...])
             dg_ref[...] += dot(mixed, c_ref[rows, :], TN)
 
-        part[...] = dg_ref[...].reshape(32, 8, D)
-        yield from all_reduce(net, *ar2)
-        dg_ref[...] = full[...].reshape(D, D)
+        ar2[0][...] = dg_ref[...].reshape(8, 32, D)
+        yield from all_reduce(net, ar2[0], None, *ar2[2:])
+        dg_ref[...] = ar2[6][...].reshape(D, D)
 
     once_t = ready(load_t)
-    drive(
-        scatter_half(net, t_hbm, t, 0, leaf.at[0], main.at[0], leaf2.at[0], main2.at[0], once_t),
-        scatter_half(net, t_hbm, t, HALF, leaf.at[1], main.at[1], leaf2.at[1], main2.at[1], once_t),
-        graph(),
-        attention(),
-    )
-
-    @pl.loop(0, NODE // CH)
-    def _(i):
-        rows = pl.ds(pl.multiple_of(i * CH, CH), CH)
-        gx_ref[rows, :] += dot(t[net.r, rows, :], wg_ref[...], NT)
-
+
+    def half(i):
+        return scatter_half(
+            net, t_hbm, t, i * HALF, leaf.at[i], main.at[i], leaf2.at[i], main2.at[i], own_ref, once_t
+        )
+
+    drive(SCATTER_ORDER, a=half(0), b=half(1), g=graph(), t=attention())
     net.finish()
 
 
@@ -661,9 +667,9 @@
     vmem, hbm = pl.BlockSpec(memory_space=pltpu.VMEM), pl.BlockSpec(memory_space=pl.ANY)
     return pl.pallas_call(
         scatter_kernel,
-        out_shape=[block, block, weight, weight, weight, weight],
+        out_shape=[block, block, block, weight, weight, weight, weight],
         in_specs=[vmem] * 12 + [hbm] * 2,
-        out_specs=[vmem] * 6,
+        out_specs=[vmem] * 7,
         scratch_shapes=[
             pltpu.VMEM((8, NODE, D), F32),
             pltpu.VMEM((16, NODE, D), F32),
@@ -678,8 +684,8 @@
             pltpu.SemaphoreType.DMA((copies,)),
             pltpu.SemaphoreType.DMA((copies,)),
         ]
-        + reduce_scratch(24)
-        + reduce_scratch(8),
+        + reduce_scratch(96, 0)
+        + reduce_scratch(32, 0),
         compiler_params=pltpu.CompilerParams(
             collective_id=1, has_side_effects=True, vmem_limit_bytes=60 * 2**20
         ),
@@ -687,11 +693,51 @@
     )(x, cot, wq, wk, wv, wg, att, gq, key, val, gs, gks, f, t)
 
 
+def finish_kernel(own_hbm, wg_ref, *refs):
+    taken, given, held, (own, load_sem, store_sem) = refs[:6], refs[6:12], refs[12:18], refs[18:]
+    loads = [pltpu.make_async_copy(own_hbm, own, load_sem.at[6])]
+    for i in range(6):
+        loads.append(pltpu.make_async_copy(taken[i], held[i], load_sem.at[i]))
+    for copy in loads:
+        copy.start()
+    stores = [pltpu.make_async_copy(held[i], given[i], store_sem.at[i]) for i in range(6)]
+    loads[0].wait()
+    term = dot(own[...], wg_ref[...], NT)
+    loads[1].wait()
+    held[0][...] += term
+    stores[0].start()
+    for i in range(1, 6):
+        loads[i + 1].wait()
+        stores[i].start()
+    for copy in stores:
+        copy.wait()
+
+
+def run_finish(own, wg, out, gx, *weights):
+    vmem, hbm = pl.BlockSpec(memory_space=pltpu.VMEM), pl.BlockSpec(memory_space=pl.ANY)
+    gx, out, *weights = pl.pallas_call(
+        finish_kernel,
+        out_shape=[jax.ShapeDtypeStruct(a.shape, F32) for a in (gx, out, *weights)],
+        in_specs=[hbm, vmem] + [hbm] * 6,
+        out_specs=[hbm] * 6,
+        scratch_shapes=[
+            *[pltpu.VMEM(a.shape, F32) for a in (gx, out, *weights)],
+            pltpu.VMEM((NODE, D), F32),
+            pltpu.SemaphoreType.DMA((7,)),
+            pltpu.SemaphoreType.DMA((6,)),
+        ],
+        compiler_params=pltpu.CompilerParams(vmem_limit_bytes=60 * 2**20),
+        name="finish",
+    )(own, wg, gx, out, *weights)
+    return (out, gx, *weights)
+
+
 def per_device(x, cot, wq, wk, wv, wg, tiles, tile_rows, tile_cols, tile_count):
     xs, cs, att, gq, key, val, gs, gks = run_gather(x, cot, wq, wk, wv)
     f, t = run_tiles(tile_rows, tile_cols, tile_count, tiles, xs, cs)
     f, t = f.reshape(8, NODE, D), t.reshape(16, NODE, D)
-    return tuple(run_scatter(x, cot, wq, wk, wv, wg, att, gq, key, val, gs, gks, f, t))
+    own, *results = run_scatter(x, cot, wq, wk, wv, wg, att, gq, key, val, gs, gks, f, t)
+    return run_finish(own, wg, *results)
 
 
 def solution(mesh):

time: 267 us -> 216 us (0.81)
  Pallas kernels: 254 us -> 214 us
  local copies, waits for them, and re-layouts: 10.8 us -> 0 us
    pallas_call x1 -> x2, Pallas kernels: 114 us -> 89.1 us  [the longest x1 84.8 us: run_scatter(): pl.pallas_call(scatter_kernel, out_shape=[block, block, block, weight, we...]
    pallas_call x1, Pallas kernels: 104 us -> 83.8 us  [run_gather(): pl.pallas_call(gather_kernel, out_shape=[jax.ShapeDtypeStruct((16, BLK, 2...]
    unnamed x6 -> x0, local copies, waits for them, and re-layouts: 10.8 us -> none
    pallas_call x1, Pallas kernels: 37 us -> 41.4 us  [run_tiles(): pl.pallas_call(tile_kernel, out_shape=[jax.ShapeDtypeStruct((8 * BLK, TIL...]
where the time goes in v2:
time: 216 us
  Pallas kernels  214 us (99%)
    pallas_call x1, Pallas kernels, run_scatter(): pl.pallas_call(scatter_kernel, out_shape=[block, block, block, weight, we...  84.8 us
    pallas_call x1, Pallas kernels, run_gather(): pl.pallas_call(gather_kernel, out_shape=[jax.ShapeDtypeStruct((16, BLK, 2...  83.8 us
    pallas_call x1, Pallas kernels, run_tiles(): pl.pallas_call(tile_kernel, out_shape=[jax.ShapeDtypeStruct((8 * BLK, TIL...  41.4 us

profile of v2, /device:TPU:1, one launch (start us, length us, event | category | flops | bytes accessed | tf_op | source)
XLA Modules:
  0.0 215.8 jit_solution(17170723706589922187)
XLA Ops:
  1.3 83.8 %gather.1 = (bf16[16,6,256,256]{3,2,1,0:T(8,128)(2,1)}, bf16[8,6,256,256]{3,2,1,0:T(8,128)(2,1)}, f32[768,256]{1,0:T(8,128)}, f32[768,256]{1,0:T(8,128)}, f32[76...) custom-call(f32[768,256]{1,0:T(8,128)} %x_ref.3, f32[768,256]{1,0:T(8,128)} %c_ref.3, ...), custom_call_target="tpu_custom_call" | custom-call | tf_op jit(solution)/shard_map/gather/pallas_call | solution.py:352
  85.1 41.4 %tiles.1 = (f32[48,128,256]{2,1,0:T(8,128)}, f32[96,128,256]{2,1,0:T(8,128)}) custom-call(s32[288]{0:T(512)} %rows_ref.1, s32[288]{0:T(512)} %cols_ref.1, s32[1]{0:T(128)S(6)} %copy.16.count_ref, f32[288,128,128]{2,1,0:T(8,128)} %tiles_ref.1, bf16[96,256,256]{2,1,0:T(8,128)(2,1)} %bitcast.5, bf16[48,256,256]{2,1,0:T(8,128)(2,1)} %bitcast.7), custom_call_target="tpu_custom_call" | custom-call | tf_op jit(solution)/shard_map/tiles/pallas_call | solution.py:455
  126.5 84.8 %scatter.1 = (f32[768,256]{1,0:T(8,128)}, f32[768,256]{1,0:T(8,128)}, f32[768,256]{1,0:T(8,128)}, f32[256,256]{1,0:T(8,128)}, f32[256,256]{1,0:T(8,128)}, /*index=5*/f32[256,256]{1,0:T(8,128)}, f32[256,256]{1,0:T(8,128)}) custom-call(f32[768,256]{1,0:T(8,128)} %x_ref.3, f32[768,256]{1,0:T(8,128)} %c_ref.3, f32[256,256]{1,0:T(8,128)} %wq_ref.3, ...), custom_call_target="tpu_custom_call" | custom-call | tf_op jit(solution)/shard_map/scatter/pallas_call | solution.py:668
  211.3 4.3 %finish.1 = (f32[768,256]{1,0:T(8,128)}, f32[768,256]{1,0:T(8,128)}, f32[256,256]{1,0:T(8,128)}, f32[256,256]{1,0:T(8,128)}, f32[256,256]{1,0:T(8,128)}, /*index=5*/f32[256,256]{1,0:T(8,128)}) custom-call(f32[768,256]{1,0:T(8,128)} %get-tuple-element.39.own_hbm, f32[256,256]{1,0:T(8,128)} %wg_ref.3, f32[768,256]{1,0:T(8,128)} %get-tuple-element.40.refs_0_, ...), custom_call_target="tpu_custom_call" | custom-call | tf_op jit(solution)/shard_map/finish/pallas_call | solution.py:718

commit v3 on v2

--- a/solution.py
+++ b/solution.py
@@ -130,7 +130,7 @@
     return net.y, net.x, lambda first, then: first % 4 * 4 + then % 4
 
 
-def gather_half(net, mine, panel, base, done):
+def gather_half(net, mine, panel, base, done, keep):
     a, b, slot = row_order(net, base)
     all_rows, up, down = pl.ds(base, HALF), pl.ds(base, QUART), pl.ds(base + QUART, QUART)
 
@@ -158,15 +158,13 @@
     second[1] = pair(None, slot(a + 1, b), all_rows, b_plus, b_minus)
     done(3, 0)
     done(1, 0)
-    third = {}
 
     def pass_on(o):
         left, right = second[o]
         left.wait_recv()
-        f_up = forward(slot(a + o, b + 3), up, b_plus)
+        keep(0, o, panel.at[slot(a + o, b + 3), up])
         right.wait_recv()
-        f_down = forward(slot(a + o, b + 1), down, b_minus)
-        third[o] = (f_up, f_down)
+        keep(1, o, panel.at[slot(a + o, b + 1), down])
         done(o, 3)
         done(o, 1)
 
@@ -182,20 +180,10 @@
     yield
     pass_on(1)
     yield
-    for copy in third[0]:
-        copy.wait_recv()
-    done(0, 2)
-    yield
     pass_on(2)
-    yield
-    for o in (3, 1, 2):
-        for copy in third[o]:
-            copy.wait_recv()
-        done(o, 2)
-        yield
-
-
-GATHER_COPIES = 2 + 2 + 4 * 4
+
+
+GATHER_COPIES = 2 + 2 + 4 * 2
 
 
 def gather_cols(net, mine, panel, done):
@@ -247,37 +235,41 @@
             step(name)
 
 
-GATHER_ORDER = "abtctabotabtabtctababctababtcabtab"
+GATHER_ORDER = "abtctabotabtabtctbtaababctabctabtab"
 
 
 def gather_kernel(
     x_ref, c_ref, wq_ref, wk_ref, wv_ref,
-    xs_ref, cs_ref, att_ref, gq_ref, key_ref, val_ref, gs_ref, gks_ref,
+    xs_ref, cs_ref, last0, last1, last2, last3, att_ref, gq_ref, key_ref, val_ref, gs_ref, gks_ref,
     q_ref, xp, cp, x_stage, c_stage, stage_sem, ssem, rsem, *reduce_refs,
 ):
     net = Net(ssem, rsem)
     net.barrier()
+    last_refs = (last0, last1, last2, last3)
     ar1, ar2 = reduce_refs[:7], reduce_refs[7:]
     staged = []
 
-    def split_out(source, stage, out, slot):
-        @pl.loop(0, BLK)
+    def send_out(source, target):
+        copy = pltpu.make_async_copy(source, target, stage_sem.at[len(staged)])
+        copy.start()
+        staged.append(copy)
+
+    def split_out(source, stage, out, slot, first=0, blocks=BLK):
+        @pl.loop(first, first + blocks)
         def _(i):
             hi, lo = split2(source[pl.ds(pl.multiple_of(i * TILE, TILE), TILE), :])
             stage[slot, i, 0:TILE, :] = hi
             stage[slot, i, TILE : 2 * TILE, :] = lo
 
-        copy = pltpu.make_async_copy(stage.at[slot], out.at[slot], stage_sem.at[len(staged)])
-        copy.start()
-        staged.append(copy)
-
-    seen = set()
-
-    def x_done(dx, dy):
-        if (dx, dy) in seen:
-            slot = (net.y + dy) % 4 * 4 + (net.x + dx) % 4
-            split_out(xp.at[slot], x_stage, xs_ref, slot)
-        seen.add((dx, dy))
+        at = pl.ds(first, blocks)
+        send_out(stage.at[slot, at], out.at[slot, at])
+
+    def x_done(half, dx, dy):
+        slot = (net.y + dy) % 4 * 4 + (net.x + dx) % 4
+        split_out(xp.at[slot], x_stage, xs_ref, slot, half * BLK // 2, BLK // 2)
+
+    def keep(half):
+        return lambda way, o, source: send_out(source, last_refs[2 * half + way].at[o])
 
     def cols_done(slot):
         split_out(cp.at[slot], c_stage, cs_ref, slot)
@@ -334,8 +326,8 @@
 
     drive(
         GATHER_ORDER,
-        a=gather_half(net, x_ref, xp, 0, x_done),
-        b=gather_half(net, x_ref, xp, HALF, lambda dy, dx: x_done(dx, dy)),
+        a=gather_half(net, x_ref, xp, 0, lambda dx, dy: x_done(0, dx, dy), keep(0)),
+        b=gather_half(net, x_ref, xp, HALF, lambda dy, dx: x_done(1, dx, dy), keep(1)),
         c=gather_cols(net, c_ref, cp, cols_done),
         t=attention(),
         o=own_blocks(),
@@ -354,19 +346,20 @@
         out_shape=[
             jax.ShapeDtypeStruct((16, BLK, 2 * TILE, D), BF16),
             jax.ShapeDtypeStruct((8, BLK, 2 * TILE, D), BF16),
+            *[jax.ShapeDtypeStruct((4, QUART, D), F32)] * 4,
             block, block, block, block,
             jax.ShapeDtypeStruct((D, D), F32),
             jax.ShapeDtypeStruct((8, D), F32),
         ],
         in_specs=[vmem] * 5,
-        out_specs=[hbm, hbm] + [vmem] * 6,
+        out_specs=[hbm] * 6 + [vmem] * 6,
         scratch_shapes=[
             pltpu.VMEM((NODE, D), F32),
             pltpu.VMEM((16, NODE, D), F32),
             pltpu.VMEM((8, NODE, D), F32),
             pltpu.VMEM((16, BLK, 2 * TILE, D), BF16),
             pltpu.VMEM((8, BLK, 2 * TILE, D), BF16),
-            pltpu.SemaphoreType.DMA((24,)),
+            pltpu.SemaphoreType.DMA((2 * 11 + 16 + 9,)),
             pltpu.SemaphoreType.DMA((copies,)),
             pltpu.SemaphoreType.DMA((copies,)),
         ]
@@ -381,126 +374,181 @@
 
 CHUNK = 16
 SLOTS = 3
-GROUP = 16
-
-
-def tile_kernel(
-    rows_ref, cols_ref, count_ref, tiles_ref, xs_ref, cs_ref,
-    f_ref, t_ref,
-    xs, cs, f, t, buf, sem, tile_sem,
-):
-    count = count_ref[0]
+
+
+def sweep(count, rows_ref, cols_ref, tiles_ref, buf, tile_sem, body):
     chunks = (count + CHUNK - 1) // CHUNK
-    load_c = pltpu.make_async_copy(cs_ref, cs, sem.at[0])
-    load_x = pltpu.make_async_copy(xs_ref, xs, sem.at[1])
 
     def fetch(chunk, slot):
         return pltpu.make_async_copy(
             tiles_ref.at[pl.ds(chunk * CHUNK, CHUNK)], buf.at[slot], tile_sem.at[slot]
         )
 
-    def sweep(body):
-        for i in range(SLOTS - 1):
-            @pl.when(i < chunks)
-            def _(i=i):
-                fetch(i, i).start()
-
-        @pl.loop(0, chunks)
-        def _(chunk):
-            slot = chunk % SLOTS
-
-            @pl.when(chunk + SLOTS - 1 < chunks)
-            def _():
-                fetch(chunk + SLOTS - 1, (chunk + SLOTS - 1) % SLOTS).start()
-
-            fetch(chunk, slot).wait()
-
-            @pl.loop(0, CHUNK // GROUP)
-            def _(group):
-                first = group * GROUP
-                for i in range(GROUP):
-                    at = chunk * CHUNK + first + i
-                    tile = buf[slot, first + i]
-                    body(jnp.where(at < count, tile, 0.0), rows_ref[at], cols_ref[at])
-
-    def product(tile, panel):
-        hi, lo = split2(tile)
-        whole = jnp.dot(jnp.concatenate([hi, hi], axis=1), panel, preferred_element_type=F32)
-        return whole + jnp.dot(lo, panel[0:TILE], preferred_element_type=F32)
-
-    def backward(tile, row, col):
-        t[col] += product(tile.T, cs[row])
-
-    def forward(tile, row, col):
-        f[row] += product(tile, xs[col])
-
-    load_c.start()
-    load_x.start()
+    for i in range(SLOTS - 1):
+        @pl.when(i < chunks)
+        def _(i=i):
+            fetch(i, i).start()
+
+    @pl.loop(0, chunks)
+    def _(chunk):
+        slot = chunk % SLOTS
+
+        @pl.when(chunk + SLOTS - 1 < chunks)
+        def _():
+            fetch(chunk + SLOTS - 1, (chunk + SLOTS - 1) % SLOTS).start()
+
+        fetch(chunk, slot).wait()
+        for i in range(CHUNK):
+            at = chunk * CHUNK + i
+            tile = buf[slot, i]
+            body(jnp.where(at < count, tile, 0.0), rows_ref[at], cols_ref[at])
+
+
+def product(tile, panel):
+    hi, lo = split2(tile)
+    whole = jnp.dot(jnp.concatenate([hi, hi], axis=1), panel, preferred_element_type=F32)
+    return whole + jnp.dot(lo, panel[0:TILE], preferred_element_type=F32)
+
+
+def block_rows(block):
+    return pl.ds(pl.multiple_of(block * TILE, TILE), TILE)
+
+
+def backward_kernel(
+    rows_ref, cols_ref, count_ref, place_ref, tiles_ref, cs_ref,
+    t_ref, leaf0, leaf1, leaf2, leaf3,
+    cs, t, buf, sem, tile_sem,
+):
+    load = pltpu.make_async_copy(cs_ref, cs, sem.at[0])
+    load.start()
     t[...] = jnp.zeros_like(t)
+    load.wait()
+
+    def body(tile, row, col):
+        t[block_rows(col), :] += product(tile.T, cs[row])
+
+    sweep(count_ref[0], rows_ref, cols_ref, tiles_ref, buf, tile_sem, body)
+    y, x = place_ref[0], place_ref[1]
+    stores = [pltpu.make_async_copy(t, t_ref, sem.at[0])]
+    for kind, leaf in enumerate((leaf0, leaf1, leaf2, leaf3)):
+        for i, o in enumerate(SCATTER_TURNS):
+            dx, dy = (o, 2) if kind < 2 else (2, o)
+            slot = (y + dy) % 4 * 4 + (x + dx) % 4
+            source = t.at[pl.ds(pl.multiple_of(slot * NODE + kind * QUART, QUART), QUART)]
+            stores.append(pltpu.make_async_copy(source, leaf.at[i], sem.at[1 + 4 * kind + i]))
+    for copy in stores:
+        copy.start()
+    for copy in stores:
+        copy.wait()
+
+
+def forward_kernel(
+    rows_ref, cols_ref, count_ref, place_ref, tiles_ref, xs_ref, last0, last1, last2, last3,
+    f_ref,
+    xs, f, late, buf, sem, tile_sem,
+):
+    load = pltpu.make_async_copy(xs_ref, xs, sem.at[0])
+    loads = [
+        pltpu.make_async_copy(last, late.at[kind], sem.at[1 + kind])
+        for kind, last in enumerate((last0, last1, last2, last3))
+    ]
+    for copy in loads + [load]:
+        copy.start()
     f[...] = jnp.zeros_like(f)
-    load_c.wait()
-    sweep(backward)
-    store_t = pltpu.make_async_copy(t, t_ref, sem.at[2])
-    store_t.start()
-    load_x.wait()
-    sweep(forward)
-    store_f = pltpu.make_async_copy(f, f_ref, sem.at[3])
-    store_f.start()
-    store_t.wait()
-    store_f.wait()
-
-
-def run_tiles(tile_rows, tile_cols, tile_count, tiles, xs, cs):
-    hbm, smem = pl.BlockSpec(memory_space=pl.ANY), pl.BlockSpec(memory_space=pltpu.SMEM)
+    for copy in loads + [load]:
+        copy.wait()
+    y, x = place_ref[0], place_ref[1]
+    for kind in range(4):
+        for o in range(4):
+            dx, dy = (o, 2) if kind < 2 else (2, o)
+            slot = (y + dy) % 4 * 4 + (x + dx) % 4
+            for part in range(0, QUART, PART):
+                block, at = divmod(kind * QUART + part, TILE)
+                hi, lo = split2(late[kind, o, part : part + PART, :])
+                xs[slot * BLK + block, at : at + PART, :] = hi
+                xs[slot * BLK + block, TILE + at : TILE + at + PART, :] = lo
+
+    def body(tile, row, col):
+        f[block_rows(row), :] += product(tile, xs[col])
+
+    sweep(count_ref[0], rows_ref, cols_ref, tiles_ref, buf, tile_sem, body)
+    store = pltpu.make_async_copy(f, f_ref, sem.at[0])
+    store.start()
+    store.wait()
+
+
+PART = 64
+SCATTER_TURNS = (2, 1, 3, 0)
+
+
+def run_sweep(kernel, name, out_shape, scratch, sems, scalars, tiles, *panels):
+    hbm, smem = pl.BlockSpec(memory_space=pltpu.HBM), pl.BlockSpec(memory_space=pltpu.SMEM)
     return pl.pallas_call(
-        tile_kernel,
-        out_shape=[
-            jax.ShapeDtypeStruct((8 * BLK, TILE, D), F32),
-            jax.ShapeDtypeStruct((16 * BLK, TILE, D), F32),
-        ],
-        in_specs=[smem] * 3 + [hbm] * 3,
-        out_specs=[hbm] * 2,
-        scratch_shapes=[
-            pltpu.VMEM((16 * BLK, 2 * TILE, D), BF16),
-            pltpu.VMEM((8 * BLK, 2 * TILE, D), BF16),
-            pltpu.VMEM((8 * BLK, TILE, D), F32),
-            pltpu.VMEM((16 * BLK, TILE, D), F32),
+        kernel,
+        out_shape=out_shape,
+        in_specs=[smem] * 4 + [hbm] * (1 + len(panels)),
+        out_specs=[hbm] * len(out_shape),
+        scratch_shapes=scratch
+        + [
             pltpu.VMEM((SLOTS, CHUNK, TILE, TILE), F32),
-            pltpu.SemaphoreType.DMA((4,)),
+            pltpu.SemaphoreType.DMA((sems,)),
             pltpu.SemaphoreType.DMA((SLOTS,)),
         ],
+        cost_estimate=pl.CostEstimate(
+            flops=12 * MAXT * TILE * TILE * D, bytes_accessed=60 * 2**20, transcendentals=0
+        ),
         compiler_params=pltpu.CompilerParams(vmem_limit_bytes=60 * 2**20),
-        name="tiles",
-    )(
-        tile_rows, tile_cols, tile_count, tiles,
-        xs.reshape(16 * BLK, 2 * TILE, D), cs.reshape(8 * BLK, 2 * TILE, D),
+        name=name,
+    )(*scalars, tiles, *panels)
+
+
+def run_backward(scalars, tiles, cs):
+    leaf = jax.ShapeDtypeStruct((4, QUART, D), F32)
+    return run_sweep(
+        backward_kernel, "backward",
+        [jax.ShapeDtypeStruct((16 * NODE, D), F32)] + [leaf] * 4,
+        [pltpu.VMEM((8 * BLK, 2 * TILE, D), BF16), pltpu.VMEM((16 * NODE, D), F32)],
+        17, scalars, tiles, cs.reshape(8 * BLK, 2 * TILE, D),
     )
 
 
-def scatter_half(net, t_hbm, t, base, leaf, main, leaf2, main2, own_ref, ready):
+def run_forward(scalars, tiles, xs, late):
+    return run_sweep(
+        forward_kernel, "forward",
+        [jax.ShapeDtypeStruct((8 * NODE, D), F32)],
+        [
+            pltpu.VMEM((16 * BLK, 2 * TILE, D), BF16),
+            pltpu.VMEM((8 * NODE, D), F32),
+            pltpu.VMEM((4, 4, QUART, D), F32),
+        ],
+        5, scalars, tiles, xs.reshape(16 * BLK, 2 * TILE, D), *late,
+    )[0]
+
+
+def ring_sends(arrays):
+    ways = ((1, 0), (3, 0), (0, 1), (0, 3))
+    sent = []
+    for array, (dy, dx) in zip(arrays, ways):
+        pairs = [(y * 4 + x, (y + dy) % 4 * 4 + (x + dx) % 4) for y in range(4) for x in range(4)]
+        sent.append(lax.ppermute(array, "rows", pairs))
+    return sent
+
+
+def scatter_half(net, t, base, leaf, main, leaf2, main2, own_ref, need):
     s, b, slot = row_order(net, base)
     up, down, both = pl.ds(base, QUART), pl.ds(base + QUART, QUART), pl.ds(base, HALF)
-    order = (2, 1, 3, 0)
+    order = SCATTER_TURNS
     b_plus, b_minus = slot(s, b + 1), slot(s, b + 3)
-    leaves, mains = [], []
-    for i, o in enumerate(order):
-        at = slot(s + o, b + 2)
-        leaves.append(
-            (
-                net.send(t_hbm.at[at, up], leaf.at[i, 0], row=b_plus),
-                net.send(t_hbm.at[at, down], leaf.at[i, 1], row=b_minus),
-            )
-        )
-        if i == 1:
-            yield
+    mains = []
     s_plus, s_minus = slot(s + 1, b), slot(s + 3, b)
 
     def main_sends(i):
-        for copy in leaves[i]:
-            copy.wait_recv()
-        plus, minus = slot(s + order[i], b + 1), slot(s + order[i], b + 3)
-        t[plus, up] += leaf[i, 0]
-        t[minus, down] += leaf[i, 1]
+        o = order[i]
+        plus, minus = slot(s + o, b + 1), slot(s + o, b + 3)
+        need(o, 1)
+        need(o, 3)
+        t[plus, up] += leaf[0, i]
+        t[minus, down] += leaf[1, i]
         return (
             net.send(t.at[plus, both], main.at[i, 0], row=b_plus),
             net.send(t.at[minus, both], main.at[i, 1], row=b_minus),
@@ -510,11 +558,10 @@
         for copy in mains[i]:
             copy.wait_recv()
         at = slot(s + order[i], b)
+        need(order[i], 0)
         t[at, both] += main[i, 0] + main[i, 1]
         return at
 
-    yield
-    ready()
     mains.append(main_sends(0))
     yield
     mains.append(main_sends(1))
@@ -548,7 +595,7 @@
     own_ref[both, :] = t[slot(s, b), both] + (main2[0] + main2[1])
 
 
-SCATTER_COPIES = GATHER_COPIES
+SCATTER_COPIES = 4 * 2 + 2 + 2
 
 
 def scatter_cols(net, f_hbm, f, pair, leaf, main, ready):
@@ -560,10 +607,10 @@
         for i, o in enumerate(order)
     ]
     yield
-    ready()
     plus, minus = (z + 1) % 4 * 2 + k, (z + 3) % 4 * 2 + k
     for i, o in enumerate(order):
         copies[i].wait_recv()
+        ready(o)
         at = (z + o) % 4 * 2 + k
         f[at] += pair[i]
         if o == 2:
@@ -590,31 +637,42 @@
 SCATTER_COLS_COPIES = 4 + 2 + 2
 
 
-SCATTER_ORDER = "abgtabttgabgtabgtababtabgabtgabgabgabg"
+SCATTER_ORDER = "gabgtabttggababtabtgababtggabtgabg"
+
+
+T_ORDER = [(2, 1), (2, 3), (1, 2), (3, 2), (1, 1), (1, 3), (3, 1), (3, 3), (2, 0), (0, 2)]
+T_ORDER += [(0, 1), (0, 3), (1, 0), (3, 0), (0, 0), (2, 2)]
 
 
 def scatter_kernel(
     x_ref, c_ref, wq_ref, wk_ref, wv_ref, wg_ref,
-    att_ref, gq_ref, key_ref, val_ref, gs_ref, gks_ref, f_hbm, t_hbm,
+    att_ref, gq_ref, key_ref, val_ref, gs_ref, gks_ref, f_hbm, t_hbm, first0, first1, first2, first3,
     own_ref, out_ref, gx_ref, dq_ref, dk_ref, dv_ref, dg_ref,
     f, t, leaf, main, leaf2, main2, pair, zleaf, zmain, load_sem, ssem, rsem, *reduce_refs,
 ):
     net = Net(ssem, rsem)
-    load_t = pltpu.make_async_copy(t_hbm, t, load_sem.at[0])
-    load_f = pltpu.make_async_copy(f_hbm, f, load_sem.at[1])
-    load_t.start()
-    load_f.start()
+    loads = {}
+
+    def load(key, source, target):
+        loads[key] = pltpu.make_async_copy(source, target, load_sem.at[len(loads)])
+        loads[key].start()
+
+    for i, first in enumerate((first0, first1, first2, first3)):
+        load(i, first, leaf.at[i // 2, i % 2])
+    for i, (dx, dy) in enumerate(T_ORDER):
+        slot = (net.y + dy) % 4 * 4 + (net.x + dx) % 4
+        load((dx, dy), t_hbm.at[slot], t.at[slot])
+        if i == 3:
+            for o in (2, 1, 3, 0):
+                at = (net.z + o) % 4 * 2 + net.k
+                load(("f", o), f_hbm.at[at], f.at[at])
     net.barrier()
     ar1, ar2 = reduce_refs[:7], reduce_refs[7:]
 
-    def ready(copy):
-        pending = [copy]
-
-        def once():
-            if pending:
-                pending.pop().wait()
-
-        return once
+    def need(*keys):
+        for key in keys:
+            if key in loads:
+                loads.pop(key).wait()
 
     def attention():
         for i in range(NODE // CH):
@@ -636,7 +694,7 @@
             grad[...] = ar1[6][:, pl.ds(32 * j, 32), :].reshape(D, D)
 
     def graph():
-        yield from scatter_cols(net, f_hbm, f, pair, zleaf, zmain, ready(load_f))
+        yield from scatter_cols(net, f_hbm, f, pair, zleaf, zmain, lambda o: need(("f", o)))
         dg_ref[...] = jnp.zeros((D, D), F32)
 
         @pl.loop(0, NODE // CH)
@@ -650,37 +708,37 @@
         yield from all_reduce(net, ar2[0], None, *ar2[2:])
         dg_ref[...] = ar2[6][...].reshape(D, D)
 
-    once_t = ready(load_t)
-
     def half(i):
-        return scatter_half(
-            net, t_hbm, t, i * HALF, leaf.at[i], main.at[i], leaf2.at[i], main2.at[i], own_ref, once_t
-        )
+        def wanted(small, big):
+            need(0, 1, 2, 3, (small, big) if i == 0 else (big, small))
+
+        return scatter_half(net, t, i * HALF, leaf.at[i], main.at[i], leaf2.at[i], main2.at[i], own_ref, wanted)
 
     drive(SCATTER_ORDER, a=half(0), b=half(1), g=graph(), t=attention())
+    need(*list(loads))
     net.finish()
 
 
-def run_scatter(x, cot, wq, wk, wv, wg, att, gq, key, val, gs, gks, f, t):
+def run_scatter(x, cot, wq, wk, wv, wg, att, gq, key, val, gs, gks, f, t, firsts):
     copies = 2 * SCATTER_COPIES + SCATTER_COLS_COPIES + 2 * REDUCE_COPIES
     block, weight = jax.ShapeDtypeStruct((NODE, D), F32), jax.ShapeDtypeStruct((D, D), F32)
-    vmem, hbm = pl.BlockSpec(memory_space=pltpu.VMEM), pl.BlockSpec(memory_space=pl.ANY)
+    vmem, hbm = pl.BlockSpec(memory_space=pltpu.VMEM), pl.BlockSpec(memory_space=pltpu.HBM)
     return pl.pallas_call(
         scatter_kernel,
         out_shape=[block, block, block, weight, weight, weight, weight],
-        in_specs=[vmem] * 12 + [hbm] * 2,
+        in_specs=[vmem] * 12 + [hbm] * 6,
         out_specs=[vmem] * 7,
         scratch_shapes=[
             pltpu.VMEM((8, NODE, D), F32),
             pltpu.VMEM((16, NODE, D), F32),
-            pltpu.VMEM((2, 4, 2, QUART, D), F32),
+            pltpu.VMEM((2, 2, 4, QUART, D), F32),
             pltpu.VMEM((2, 4, 2, HALF, D), F32),
             pltpu.VMEM((2, 2, QUART, D), F32),
             pltpu.VMEM((2, 2, HALF, D), F32),
             pltpu.VMEM((4, NODE, D), F32),
             pltpu.VMEM((2, HALF, D), F32),
             pltpu.VMEM((2, NODE, D), F32),
-            pltpu.SemaphoreType.DMA((2,)),
+            pltpu.SemaphoreType.DMA((24,)),
             pltpu.SemaphoreType.DMA((copies,)),
             pltpu.SemaphoreType.DMA((copies,)),
         ]
@@ -690,7 +748,7 @@
             collective_id=1, has_side_effects=True, vmem_limit_bytes=60 * 2**20
         ),
         name="scatter",
-    )(x, cot, wq, wk, wv, wg, att, gq, key, val, gs, gks, f, t)
+    )(x, cot, wq, wk, wv, wg, att, gq, key, val, gs, gks, f, t, *firsts)
 
 
 def finish_kernel(own_hbm, wg_ref, *refs):
@@ -733,10 +791,16 @@
 
 
 def per_device(x, cot, wq, wk, wv, wg, tiles, tile_rows, tile_cols, tile_count):
-    xs, cs, att, gq, key, val, gs, gks = run_gather(x, cot, wq, wk, wv)
-    f, t = run_tiles(tile_rows, tile_cols, tile_count, tiles, xs, cs)
-    f, t = f.reshape(8, NODE, D), t.reshape(16, NODE, D)
-    own, *results = run_scatter(x, cot, wq, wk, wv, wg, att, gq, key, val, gs, gks, f, t)
+    xs, cs, *rest = run_gather(x, cot, wq, wk, wv)
+    last, (att, gq, key, val, gs, gks) = rest[:4], rest[4:]
+    row = lax.axis_index("rows")
+    scalars = (tile_rows, tile_cols, tile_count, jnp.stack([row // 4, row % 4]))
+    late = ring_sends(last)
+    t, *leaves = run_backward(scalars, tiles, cs)
+    firsts = ring_sends(leaves)
+    f = run_forward(scalars, tiles, xs, late).reshape(8, NODE, D)
+    t = t.reshape(16, NODE, D)
+    own, *results = run_scatter(x, cot, wq, wk, wv, wg, att, gq, key, val, gs, gks, f, t, firsts)
     return run_finish(own, wg, *results)
 
 

time: 216 us -> 211 us (0.977)
  Pallas kernels: 214 us -> 194 us
  starting transfers between devices: 0 us -> 10.8 us
  local copies, waits for them, and re-layouts: 0 us -> 3.39 us
    pallas_call x1, Pallas kernels: 84.8 us -> 71 us  [run_scatter(): pl.pallas_call(scatter_kernel, out_shape=[block, block, block, weight, we...]
    pallas_call x1, Pallas kernels: 83.8 us -> 70.7 us  [run_gather(): pl.pallas_call(gather_kernel, out_shape=[jax.ShapeDtypeStruct((16, BLK, 2...]
    ppermute x0 -> x8, starting transfers between devices: none -> 10.8 us  [ring_sends(): sent.append(lax.ppermute(array, 'rows', pairs))]
    pallas_call x1 -> x2, Pallas kernels: 41.4 us -> 48.1 us  [run_sweep(): pl.pallas_call(kernel, out_shape=out_shape, in_specs=[smem] * 4 + [hbm] *...]
    unnamed x0 -> x14, local copies, waits for them, and re-layouts: none -> 3.39 us
  transfers between devices with their start and end apart: 0 -> 8, of which waited for: 0 -> 0; matrix products, arithmetic and copies ran while one was open for 0% -> 0% of each run, Pallas kernels for 0% -> 23%
where the time goes in v3:
time: 211 us; the launch traced here: 210 us
  Pallas kernels  194 us (92%)
  starting transfers between devices  10.8 us (5%)
  local copies, waits for them, and re-layouts  3.39 us (2%)
    pallas_call x1, Pallas kernels, run_scatter(): pl.pallas_call(scatter_kernel, out_shape=[block, block, block, weight, we...  71 us
    pallas_call x1, Pallas kernels, run_gather(): pl.pallas_call(gather_kernel, out_shape=[jax.ShapeDtypeStruct((16, BLK, 2...  70.7 us
    pallas_call x2, Pallas kernels, run_sweep(): pl.pallas_call(kernel, out_shape=out_shape, in_specs=[smem] * 4 + [hbm] *...  48.1 us
    ppermute x8, starting transfers between devices, ring_sends(): sent.append(lax.ppermute(array, 'rows', pairs))  10.8 us
    pallas_call x1, Pallas kernels, run_finish(): pl.pallas_call(finish_kernel, out_shape=[jax.ShapeDtypeStruct(a.shape, F3...  4.27 us
  transfers between devices with their start and end apart: 8, of which 0 were waited for; matrix products, arithmetic and copies ran while one was open for 0% of the time, Pallas kernels for 23%

profile of v3, /device:TPU:1, one launch (start us, length us, event | category | flops | bytes accessed | tf_op | source)
XLA Modules:
  0.0 210.5 jit_solution(15353473904622214665)
XLA Ops:
  0.6 70.7 %gather.1 = (bf16[16,6,256,256]{3,2,1,0:T(8,128)(2,1)}, bf16[8,6,256,256]{3,2,1,0:T(8,128)(2,1)}, f32[4,192,256]{2,1,0:T(8,128)}, f32[4,192,256]{2,1,0:T(8,128)}...) custom-call(f32[768,256]{1,0:T(8,128)} %x_ref.3, ...), custom_call_target="tpu_custom_call" | custom-call | tf_op jit(solution)/shard_map/gather/pallas_call | solution.py:344
  71.4 0.1 collective-permute-start
  71.5 2.6 %collective-permute-start.1 = (f32[4,192,256]{2,1,0:T(8,128)}, f32[4,192,256]{2,1,0:T(8,128)S(1)}, u32[]{:S(2)}, u32[]{:S(2)}) collective-permute-start(f32[4,192,256]{2,1,0:T(8,128)} %get-tuple-element.44), channel_id=1, source_target_pairs={{0,96},{8,104},{16,112},{24,120},{32,0},{40,8},{48,16},{56,24},{64... | collective-permute-start | bytes 2359304 | tf_op jit(solution)/shard_map/ppermute | solution.py:533
  74.1 0.4 collective-permute-start.2
  74.5 2.2 %collective-permute-start.3 = (f32[4,192,256]{2,1,0:T(8,128)}, f32[4,192,256]{2,1,0:T(8,128)}, u32[]{:S(2)}, u32[]{:S(2)}) collective-permute-start(f32[4,192,256]{2,1,0:T(8,128)} %get-tuple-element.46), channel_id=1, source_target_pairs={{0,24},{8,0},{16,8},{24,16},{32,56},{40,32},{48,40},{56,48},{64,88... | collective-permute-start | bytes 2359304 | tf_op jit(solution)/shard_map/ppermute | solution.py:533
  77.4 0.6 pad_add_fusion.place_ref
  78.0 24.5 %backward.1 = (f32[12288,256]{1,0:T(8,128)}, f32[4,192,256]{2,1,0:T(8,128)}, f32[4,192,256]{2,1,0:T(8,128)}, f32[4,192,256]{2,1,0:T(8,128)}, f32[4,192,256]{2,1,0:T(8,128)}) custom-call(s32[288]{0:T(512)} %rows_ref.3, s32[288]{0:T(512)} %cols_ref.3, s32[1]{0:T(128)S(6)} %copy.16.count_ref, s32[2]{0:T(128)} %pad_add_fusion.place_ref, ...), custom_call_target="tpu_custom_call" | custom-call | flops 14495514624 | bytes 62914560 | tf_op jit(solution)/shard_map/backward/pallas_call | solution.py:486
  102.5 0.1 collective-permute-start.4
  102.6 0.0 copy-start.4
  102.7 2.6 %collective-permute-start.5 = (f32[4,192,256]{2,1,0:T(8,128)}, f32[4,192,256]{2,1,0:T(8,128)S(1)}, u32[]{:S(2)}, u32[]{:S(2)}) collective-permute-start(f32[4,192,256]{2,1,0:T(8,128)} %get-tuple-element.50), channel_id=1, source_target_pairs={{0,96},{8,104},{16,112},{24,120},{32,0},{40,8},{48,16},{56,24},{64... | collective-permute-start | bytes 2359304 | tf_op jit(solution)/shard_map/ppermute | solution.py:533
  105.3 0.9 copy-done.5
  106.2 0.0 collective-permute-start.6
  106.2 0.0 collective-permute-done.2.last2
  106.2 0.9 copy-done.6
  107.1 2.7 %collective-permute-start.7 = (f32[4,192,256]{2,1,0:T(8,128)}, f32[4,192,256]{2,1,0:T(8,128)S(1)}, u32[]{:S(2)}, u32[]{:S(2)}) collective-permute-start(f32[4,192,256]{2,1,0:T(8,128)} %get-tuple-element.52), channel_id=1, source_target_pairs={{0,24},{8,0},{16,8},{24,16},{32,56},{40,32},{48,40},{56,48},{64,88... | collective-permute-start | bytes 2359304 | tf_op jit(solution)/shard_map/ppermute | solution.py:533
  109.8 23.6 %forward.1 = f32[6144,256]{1,0:T(8,128)} custom-call(s32[288]{0:T(512)} %rows_ref.3, s32[288]{0:T(512)} %cols_ref.3, s32[1]{0:T(128)S(6)} %copy.16.count_ref, s32[2]{0:T(128)} %pad_add_fusion.place_ref, f32[288,128,128]{2,1,0:T(8,128)} %tiles_ref.3, bf16[96,256,256]{2,1,0:T(8,128)(2,1)} %bitcast.8, f32[4,192,256]{2,1,0:T(8,128)} %copy-done.4, ...), custom_call_target="tpu_custom_call" | custom-call | flops 14495514624 | bytes 62914560 | tf_op jit(solution)/shard_map/forward/pallas_call | solution.py:486
  133.3 0.0 copy-start
  133.4 0.0 copy-start.1
  133.4 0.8 copy-done
  134.2 0.3 copy-done.1
  134.5 0.3 copy-done.2
  134.8 0.2 copy-done.3
  135.0 71.0 %scatter.1 = (f32[768,256]{1,0:T(8,128)}, f32[768,256]{1,0:T(8,128)}, f32[768,256]{1,0:T(8,128)}, f32[256,256]{1,0:T(8,128)}, f32[256,256]{1,0:T(8,128)}, /*index=5*/f32[256,256]{1,0:T(8,128)}, f32[256,256]{1,0:T(8,128)}) custom-call(f32[768,256]{1,0:T(8,128)} %x_ref.3, f32[768,256]{1,0:T(8,128)} %c_ref.3, f32[256,256]{1,0:T(8,128)} %wq_ref.3, ...), custom_call_target="tpu_custom_call" | custom-call | tf_op jit(solution)/shard_map/scatter/pallas_call | solution.py:726
  206.0 4.3 %finish.1 = (f32[768,256]{1,0:T(8,128)}, f32[768,256]{1,0:T(8,128)}, f32[256,256]{1,0:T(8,128)}, f32[256,256]{1,0:T(8,128)}, f32[256,256]{1,0:T(8,128)}, /*index=5*/f32[256,256]{1,0:T(8,128)}) custom-call(f32[768,256]{1,0:T(8,128)} %get-tuple-element.53.own_hbm, f32[256,256]{1,0:T(8,128)} %wg_ref.3, f32[768,256]{1,0:T(8,128)} %get-tuple-element.54.refs_0_, ...), custom_call_target="tpu_custom_call" | custom-call | tf_op jit(solution)/shard_map/finish/pallas_call | solution.py:776
  (12 shorter events, 0.0 us)
Async XLA Ops:
  71.4 31.3 %collective-permute-start = (f32[4,192,256]{2,1,0:T(8,128)}, f32[4,192,256]{2,1,0:T(8,128)S(1)}, u32[]{:S(2)}, u32[]{:S(2)}) collective-permute-start(f32[4,192,256]{2,1,0:T(8,128)} %get-tuple-element.43), channel_id=1, source_target_pairs={{0,32},{8,40},{16,48},{24,56},{32,64},{40,72},{48,80},{56,88},{64,... | collective-permute-start | bytes 2359304 | tf_op jit(solution)/shard_map/ppermute | solution.py:533
  71.5 33.8 %collective-permute-start.1 = (f32[4,192,256]{2,1,0:T(8,128)}, f32[4,192,256]{2,1,0:T(8,128)S(1)}, u32[]{:S(2)}, u32[]{:S(2)}) collective-permute-start(f32[4,192,256]{2,1,0:T(8,128)} %get-tuple-element.44), channel_id=1, source_target_pairs={{0,96},{8,104},{16,112},{24,120},{32,0},{40,8},{48,16},{56,24},{64... | collective-permute-start | bytes 2359304 | tf_op jit(solution)/shard_map/ppermute | solution.py:533
  74.1 32.1 %collective-permute-start.2 = (f32[4,192,256]{2,1,0:T(8,128)}, f32[4,192,256]{2,1,0:T(8,128)S(1)}, u32[]{:S(2)}, u32[]{:S(2)}) collective-permute-start(f32[4,192,256]{2,1,0:T(8,128)} %get-tuple-element.45), channel_id=1, source_target_pairs={{0,8},{8,16},{16,24},{24,0},{32,40},{40,48},{48,56},{56,32},{64,72... | collective-permute-start | bytes 2359304 | tf_op jit(solution)/shard_map/ppermute | solution.py:533
  74.5 35.2 %collective-permute-start.3 = (f32[4,192,256]{2,1,0:T(8,128)}, f32[4,192,256]{2,1,0:T(8,128)}, u32[]{:S(2)}, u32[]{:S(2)}) collective-permute-start(f32[4,192,256]{2,1,0:T(8,128)} %get-tuple-element.46), channel_id=1, source_target_pairs={{0,24},{8,0},{16,8},{24,16},{32,56},{40,32},{48,40},{56,48},{64,88... | collective-permute-start | bytes 2359304 | tf_op jit(solution)/shard_map/ppermute | solution.py:533
  102.5 30.8 %collective-permute-start.4 = (f32[4,192,256]{2,1,0:T(8,128)}, f32[4,192,256]{2,1,0:T(8,128)S(1)}, u32[]{:S(2)}, u32[]{:S(2)}) collective-permute-start(f32[4,192,256]{2,1,0:T(8,128)} %get-tuple-element.49), channel_id=1, source_target_pairs={{0,32},{8,40},{16,48},{24,56},{32,64},{40,72},{48,80},{56,88},{64,... | collective-permute-start | bytes 2359304 | tf_op jit(solution)/shard_map/ppermute | solution.py:533
  102.6 7.1 %copy-start.4 = (f32[4,192,256]{2,1,0:T(8,128)}, f32[4,192,256]{2,1,0:T(8,128)S(1)}, u32[]{:S(2)}) copy-start(f32[4,192,256]{2,1,0:T(8,128)S(1)} %collective-permute-done.last0) | copy-start | bytes 2359300
  102.7 30.7 %collective-permute-start.5 = (f32[4,192,256]{2,1,0:T(8,128)}, f32[4,192,256]{2,1,0:T(8,128)S(1)}, u32[]{:S(2)}, u32[]{:S(2)}) collective-permute-start(f32[4,192,256]{2,1,0:T(8,128)} %get-tuple-element.50), channel_id=1, source_target_pairs={{0,96},{8,104},{16,112},{24,120},{32,0},{40,8},{48,16},{56,24},{64... | collective-permute-start | bytes 2359304 | tf_op jit(solution)/shard_map/ppermute | solution.py:533
  105.3 0.9 copy-start.5
  106.2 27.2 %collective-permute-start.6 = (f32[4,192,256]{2,1,0:T(8,128)}, f32[4,192,256]{2,1,0:T(8,128)S(1)}, u32[]{:S(2)}, u32[]{:S(2)}) collective-permute-start(f32[4,192,256]{2,1,0:T(8,128)} %get-tuple-element.51), channel_id=1, source_target_pairs={{0,8},{8,16},{16,24},{24,0},{32,40},{40,48},{48,56},{56,32},{64,72... | collective-permute-start | bytes 2359304 | tf_op jit(solution)/shard_map/ppermute | solution.py:533
  106.2 0.9 copy-start.6
  107.1 26.3 %collective-permute-start.7 = (f32[4,192,256]{2,1,0:T(8,128)}, f32[4,192,256]{2,1,0:T(8,128)S(1)}, u32[]{:S(2)}, u32[]{:S(2)}) collective-permute-start(f32[4,192,256]{2,1,0:T(8,128)} %get-tuple-element.52), channel_id=1, source_target_pairs={{0,24},{8,0},{16,8},{24,16},{32,56},{40,32},{48,40},{56,48},{64,88... | collective-permute-start | bytes 2359304 | tf_op jit(solution)/shard_map/ppermute | solution.py:533
  133.3 0.9 copy-start
  133.4 1.1 copy-start.1
  133.4 1.4 copy-start.2
  133.4 1.6 copy-start.3

commit v4 on v3

--- a/solution.py
+++ b/solution.py
@@ -71,24 +71,32 @@
             copy.wait_send()
 
 
-def all_reduce(net, part, key, r1, kbuf, r2, r3, full):
-    c, x, y = net.c, net.x, net.y
+def all_reduce(net, part, key, r0, r1, kbuf, r2, r3, full):
+    x, y, z, k = net.x, net.y, net.z, net.k
     n = part.shape[1]
-    first = [net.send(part.at[(c + j) % 8], r1.at[j - 1], col=(c + j) % 8) for j in range(1, 8)]
+    sibling = z * 2 + 1 - k
+    mine, theirs = pl.ds(k * 4, 4), pl.ds((1 - k) * 4, 4)
+    first = [net.send(part.at[theirs], r0, col=sibling)]
     if key is not None:
-        first += [net.send(key, kbuf.at[j - 1], col=(c + j) % 8) for j in range(1, 8)]
-    yield
+        kbuf[4] = key[...]
+        first.append(net.send(kbuf.at[4], kbuf.at[3], col=sibling))
     for copy in first:
         copy.wait_recv()
-    total = part[c]
-    for j in range(7):
-        total = total + r1[j]
-    r2[x, 0:n] = total
+    part[mine] += r0[...]
     if key is not None:
-        total = key[...]
-        for j in range(7):
-            total = total + kbuf[j]
-        r2[x, n:] = total
+        key[...] += kbuf[3]
+    first = []
+    for j in range(1, 4):
+        to = (z + j) % 4
+        first.append(net.send(part.at[k * 4 + to], r1.at[j - 1], col=to * 2 + k))
+        if key is not None:
+            first.append(net.send(key, kbuf.at[j - 1], col=to * 2 + k))
+    yield
+    for copy in first:
+        copy.wait_recv()
+    r2[x, 0:n] = (part[k * 4 + z] + r1[0]) + (r1[1] + r1[2])
+    if key is not None:
+        r2[x, n:] = (key[...] + kbuf[0]) + (kbuf[1] + kbuf[2])
     second = [net.send(r2.at[x], r2.at[x], row=y * 4 + (x + j) % 4) for j in range(1, 4)]
     yield
     for copy in second:
@@ -98,11 +106,13 @@
     yield
     for copy in third:
         copy.wait_recv()
-    full[c] = (r3[0, 0:n] + r3[1, 0:n]) + (r3[2, 0:n] + r3[3, 0:n])
-    fourth = [net.send(full.at[c], full.at[c], col=(c + j) % 8) for j in range(1, 8)]
+    at = k * 4 + z
+    full[at] = (r3[0, 0:n] + r3[1, 0:n]) + (r3[2, 0:n] + r3[3, 0:n])
+    fourth = [net.send(full.at[at], full.at[at], col=(z + j) % 4 * 2 + k) for j in range(1, 4)]
     yield
     for copy in fourth:
         copy.wait_recv()
+    net.send(full.at[mine], full.at[mine], col=sibling).wait_recv()
 
 
 def key_total(r3, n):
@@ -113,15 +123,16 @@
     return [
         pltpu.VMEM((8, n, D), F32),
         pltpu.VMEM((8, D), F32),
-        pltpu.VMEM((7, n, D), F32),
-        pltpu.VMEM((7, 8, D), F32),
+        pltpu.VMEM((4, n, D), F32),
+        pltpu.VMEM((3, n, D), F32),
+        pltpu.VMEM((5, 8, D), F32),
         pltpu.VMEM((4, n + extra, D), F32),
         pltpu.VMEM((4, n + extra, D), F32),
         pltpu.VMEM((8, n, D), F32),
     ]
 
 
-REDUCE_COPIES = 7 + 7 + 3 + 3 + 7
+REDUCE_COPIES = 2 + 6 + 3 + 3 + 3 + 1
 
 
 def row_order(net, base):
@@ -240,13 +251,13 @@
 
 def gather_kernel(
     x_ref, c_ref, wq_ref, wk_ref, wv_ref,
-    xs_ref, cs_ref, last0, last1, last2, last3, att_ref, gq_ref, key_ref, val_ref, gs_ref, gks_ref,
-    q_ref, xp, cp, x_stage, c_stage, stage_sem, ssem, rsem, *reduce_refs,
+    xs_ref, cs_ref, last0, last1, last2, last3, att_out, gq_out, key_out, val_out, gs_ref, gks_ref,
+    att_ref, gq_ref, key_ref, val_ref, q_ref, xp, cp, x_stage, c_stage, stage_sem, ssem, rsem, *reduce_refs,
 ):
     net = Net(ssem, rsem)
     net.barrier()
     last_refs = (last0, last1, last2, last3)
-    ar1, ar2 = reduce_refs[:7], reduce_refs[7:]
+    ar1, ar2 = reduce_refs[:8], reduce_refs[8:]
     staged = []
 
     def send_out(source, target):
@@ -289,11 +300,13 @@
 
         zero = (jnp.zeros((D, D), F32), jnp.zeros((1, D), F32))
         state, key_sum = lax.fori_loop(0, NODE // CH, first, zero)
+        send_out(key_ref, key_out)
+        send_out(val_ref, val_out)
         ar1[0][...] = state.reshape(8, 32, D)
         ar1[1][...] = jnp.broadcast_to(key_sum, (8, D))
         yield from all_reduce(net, *ar1)
-        state = ar1[6][...].reshape(D, D)
-        key_row = key_total(ar1[5], 32)[0:1]
+        state = ar1[7][...].reshape(D, D)
+        key_row = key_total(ar1[6], 32)[0:1]
 
         def second(i, sums):
             grad_state, grad_key_sum = sums
@@ -313,11 +326,13 @@
             )
 
         grad_state, grad_key_sum = lax.fori_loop(0, NODE // CH, second, zero)
+        send_out(att_ref, att_out)
+        send_out(gq_ref, gq_out)
         ar2[0][...] = grad_state.reshape(8, 32, D)
         ar2[1][...] = jnp.broadcast_to(grad_key_sum, (8, D))
         yield from all_reduce(net, *ar2)
-        gs_ref[...] = ar2[6][...].reshape(D, D)
-        gks_ref[...] = key_total(ar2[5], 32)
+        gs_ref[...] = ar2[7][...].reshape(D, D)
+        gks_ref[...] = key_total(ar2[6], 32)
 
     def own_blocks():
         yield
@@ -352,14 +367,14 @@
             jax.ShapeDtypeStruct((8, D), F32),
         ],
         in_specs=[vmem] * 5,
-        out_specs=[hbm] * 6 + [vmem] * 6,
+        out_specs=[hbm] * 10 + [vmem] * 2,
         scratch_shapes=[
-            pltpu.VMEM((NODE, D), F32),
+            *[pltpu.VMEM((NODE, D), F32)] * 5,
             pltpu.VMEM((16, NODE, D), F32),
             pltpu.VMEM((8, NODE, D), F32),
             pltpu.VMEM((16, BLK, 2 * TILE, D), BF16),
             pltpu.VMEM((8, BLK, 2 * TILE, D), BF16),
-            pltpu.SemaphoreType.DMA((2 * 11 + 16 + 9,)),
+            pltpu.SemaphoreType.DMA((2 * 11 + 16 + 9 + 4,)),
             pltpu.SemaphoreType.DMA((copies,)),
             pltpu.SemaphoreType.DMA((copies,)),
         ]
@@ -372,7 +387,7 @@
     )(x, cot, wq, wk, wv)
 
 
-CHUNK = 16
+CHUNK = 32
 SLOTS = 3
 
 
@@ -497,7 +512,7 @@
         cost_estimate=pl.CostEstimate(
             flops=12 * MAXT * TILE * TILE * D, bytes_accessed=60 * 2**20, transcendentals=0
         ),
-        compiler_params=pltpu.CompilerParams(vmem_limit_bytes=60 * 2**20),
+        compiler_params=pltpu.CompilerParams(vmem_limit_bytes=63 * 2**20),
         name=name,
     )(*scalars, tiles, *panels)
 
@@ -637,7 +652,7 @@
 SCATTER_COLS_COPIES = 4 + 2 + 2
 
 
-SCATTER_ORDER = "gabgtabttggababtabtgababtggabtgabg"
+SCATTER_ORDER = "gabgabtgabttgabtabgtabgabtgabgtg"
 
 
 T_ORDER = [(2, 1), (2, 3), (1, 2), (3, 2), (1, 1), (1, 3), (3, 1), (3, 3), (2, 0), (0, 2)]
@@ -645,9 +660,10 @@
 
 
 def scatter_kernel(
-    x_ref, c_ref, wq_ref, wk_ref, wv_ref, wg_ref,
-    att_ref, gq_ref, key_ref, val_ref, gs_ref, gks_ref, f_hbm, t_hbm, first0, first1, first2, first3,
-    own_ref, out_ref, gx_ref, dq_ref, dk_ref, dv_ref, dg_ref,
+    x_in, c_in, wq_ref, wk_ref, wv_ref, wg_ref,
+    att_in, gq_in, key_in, val_in, gs_ref, gks_ref, f_hbm, t_hbm, first0, first1, first2, first3,
+    own_ref, out_hbm, gx_hbm, dq_ref, dk_ref, dv_ref, dg_ref,
+    x_ref, c_ref, att_ref, gq_ref, key_ref, val_ref, out_ref, gx_ref, store_sem,
     f, t, leaf, main, leaf2, main2, pair, zleaf, zmain, load_sem, ssem, rsem, *reduce_refs,
 ):
     net = Net(ssem, rsem)
@@ -666,8 +682,18 @@
             for o in (2, 1, 3, 0):
                 at = (net.z + o) % 4 * 2 + net.k
                 load(("f", o), f_hbm.at[at], f.at[at])
+            load("gq", gq_in, gq_ref)
+            load("key", key_in, key_ref)
+            load("val", val_in, val_ref)
+            load("x", x_in, x_ref)
+    load("cot", c_in, c_ref)
+    load("att", att_in, att_ref)
+    stores = [
+        pltpu.make_async_copy(gx_ref, gx_hbm, store_sem.at[0]),
+        pltpu.make_async_copy(out_ref, out_hbm, store_sem.at[1]),
+    ]
     net.barrier()
-    ar1, ar2 = reduce_refs[:7], reduce_refs[7:]
+    ar1, ar2 = reduce_refs[:8], reduce_refs[8:]
 
     def need(*keys):
         for key in keys:
@@ -675,6 +701,7 @@
                 loads.pop(key).wait()
 
     def attention():
+        need("gq", "key", "val", "x")
         for i in range(NODE // CH):
             rows = pl.ds(i * CH, CH)
             x = x_ref[rows, :]
@@ -689,13 +716,15 @@
                 at = pl.ds(32 * j, 32)
                 ar1[0][:, at, :] = product if i == 0 else ar1[0][:, at, :] + product
             yield
+        stores[0].start()
         yield from all_reduce(net, ar1[0], None, *ar1[2:])
         for j, grad in enumerate((dq_ref, dk_ref, dv_ref)):
-            grad[...] = ar1[6][:, pl.ds(32 * j, 32), :].reshape(D, D)
+            grad[...] = ar1[7][:, pl.ds(32 * j, 32), :].reshape(D, D)
 
     def graph():
         yield from scatter_cols(net, f_hbm, f, pair, zleaf, zmain, lambda o: need(("f", o)))
         dg_ref[...] = jnp.zeros((D, D), F32)
+        need("cot", "att")
 
         @pl.loop(0, NODE // CH)
         def _(i):
@@ -704,9 +733,10 @@
             out_ref[rows, :] = att_ref[rows, :] + dot(mixed, wg_ref[...])
             dg_ref[...] += dot(mixed, c_ref[rows, :], TN)
 
+        stores[1].start()
         ar2[0][...] = dg_ref[...].reshape(8, 32, D)
         yield from all_reduce(net, ar2[0], None, *ar2[2:])
-        dg_ref[...] = ar2[6][...].reshape(D, D)
+        dg_ref[...] = ar2[7][...].reshape(D, D)
 
     def half(i):
         def wanted(small, big):
@@ -716,6 +746,8 @@
 
     drive(SCATTER_ORDER, a=half(0), b=half(1), g=graph(), t=attention())
     need(*list(loads))
+    for copy in stores:
+        copy.wait()
     net.finish()
 
 
@@ -726,9 +758,11 @@
     return pl.pallas_call(
         scatter_kernel,
         out_shape=[block, block, block, weight, weight, weight, weight],
-        in_specs=[vmem] * 12 + [hbm] * 6,
-        out_specs=[vmem] * 7,
+        in_specs=[hbm] * 2 + [vmem] * 4 + [hbm] * 4 + [vmem] * 2 + [hbm] * 6,
+        out_specs=[vmem] + [hbm] * 2 + [vmem] * 4,
         scratch_shapes=[
+            *[pltpu.VMEM((NODE, D), F32)] * 8,
+            pltpu.SemaphoreType.DMA((2,)),
             pltpu.VMEM((8, NODE, D), F32),
             pltpu.VMEM((16, NODE, D), F32),
             pltpu.VMEM((2, 2, 4, QUART, D), F32),
@@ -738,7 +772,7 @@
             pltpu.VMEM((4, NODE, D), F32),
             pltpu.VMEM((2, HALF, D), F32),
             pltpu.VMEM((2, NODE, D), F32),
-            pltpu.SemaphoreType.DMA((24,)),
+            pltpu.SemaphoreType.DMA((30,)),
             pltpu.SemaphoreType.DMA((copies,)),
             pltpu.SemaphoreType.DMA((copies,)),
         ]

time: 211 us -> 200 us (0.948)
  Pallas kernels: 194 us -> 177 us
  starting transfers between devices: 10.8 us -> 17.5 us
  local copies, waits for them, and re-layouts: 3.39 us -> 0.01 us
  waiting for transfers between devices: 0.02 us -> 2.2 us
    pallas_call x2, Pallas kernels: 48.1 us -> 27 us  [run_sweep(): pl.pallas_call(kernel, out_shape=out_shape, in_specs=[smem] * 4 + [hbm] *...]
    ppermute x8, starting transfers between devices: 10.8 us -> 17.5 us  [ring_sends(): sent.append(lax.ppermute(array, 'rows', pairs))]
    pallas_call x1, Pallas kernels: 71 us -> 76.6 us  [run_scatter(): pl.pallas_call(scatter_kernel, out_shape=[block, block, block, weight, we...]
    unnamed x14 -> x2, local copies, waits for them, and re-layouts: 3.39 us -> 0.01 us
    ppermute x8, waiting for transfers between devices: 0.02 us -> 2.2 us  [ring_sends(): sent.append(lax.ppermute(array, 'rows', pairs))]
  transfers between devices with their start and end apart: 8 -> 8, of which waited for: 0 -> 2; matrix products, arithmetic and copies ran while one was open for 0% -> 0% of each run, Pallas kernels for 23% -> 14%
where the time goes in v4:
time: 200 us; the launch traced here: 199 us
  Pallas kernels  177 us (88%)
  starting transfers between devices  17.5 us (9%)
  waiting for transfers between devices  2.2 us (1%)
    pallas_call x1, Pallas kernels, run_scatter(): pl.pallas_call(scatter_kernel, out_shape=[block, block, block, weight, we...  76.6 us
    pallas_call x1, Pallas kernels, run_gather(): pl.pallas_call(gather_kernel, out_shape=[jax.ShapeDtypeStruct((16, BLK, 2...  69.2 us
    pallas_call x2, Pallas kernels, run_sweep(): pl.pallas_call(kernel, out_shape=out_shape, in_specs=[smem] * 4 + [hbm] *...  27 us
    ppermute x8, starting transfers between devices, ring_sends(): sent.append(lax.ppermute(array, 'rows', pairs))  17.5 us
    pallas_call x1, Pallas kernels, run_finish(): pl.pallas_call(finish_kernel, out_shape=[jax.ShapeDtypeStruct(a.shape, F3...  4.27 us
  transfers between devices with their start and end apart: 8, of which 2 were waited for; matrix products, arithmetic and copies ran while one was open for 0% of the time, Pallas kernels for 14%

profile of v4, /device:TPU:1, one launch (start us, length us, event | category | flops | bytes accessed | tf_op | source)
XLA Modules:
  0.0 198.8 jit_solution(7460139411919773852)
XLA Ops:
  0.6 69.2 %gather.1 = (bf16[16,6,256,256]{3,2,1,0:T(8,128)(2,1)}, bf16[8,6,256,256]{3,2,1,0:T(8,128)(2,1)}, f32[4,192,256]{2,1,0:T(8,128)}, f32[4,192,256]{2,1,0:T(8,128)}...) custom-call(f32[768,256]{1,0:T(8,128)} %x_in.1, ...), custom_call_target="tpu_custom_call" | custom-call | tf_op jit(solution)/shard_map/gather/pallas_call | solution.py:359
  69.9 1.2 collective-permute-start
  71.1 1.6 collective-permute-start.1
  72.7 0.0 collective-permute-start.2
  72.7 2.7 %collective-permute-start.3 = (f32[4,192,256]{2,1,0:T(8,128)}, f32[4,192,256]{2,1,0:T(8,128)}, u32[]{:S(2)}, u32[]{:S(2)}) collective-permute-start(f32[4,192,256]{2,1,0:T(8,128)} %get-tuple-element.46), channel_id=1, source_target_pairs={{0,24},{8,0},{16,8},{24,16},{32,56},{40,32},{48,40},{56,48},{64,88... | collective-permute-start | bytes 2359304 | tf_op jit(solution)/shard_map/ppermute | solution.py:548
  76.0 0.6 pad_add_fusion.place_ref
  76.6 13.6 %backward.1 = (f32[12288,256]{1,0:T(8,128)}, f32[4,192,256]{2,1,0:T(8,128)}, f32[4,192,256]{2,1,0:T(8,128)}, f32[4,192,256]{2,1,0:T(8,128)}, f32[4,192,256]{2,1,0:T(8,128)}) custom-call(s32[288]{0:T(512)} %rows_ref.3, s32[288]{0:T(512)} %cols_ref.3, s32[1]{0:T(128)S(6)} %copy.16.count_ref, s32[2]{0:T(128)} %pad_add_fusion.place_ref, ...), custom_call_target="tpu_custom_call" | custom-call | flops 14495514624 | bytes 62914560 | tf_op jit(solution)/shard_map/backward/pallas_call | solution.py:501
  90.2 9.2 %collective-permute-start.4 = (f32[4,192,256]{2,1,0:T(8,128)}, f32[4,192,256]{2,1,0:T(8,128)S(1)}, u32[]{:S(2)}, u32[]{:S(2)}) collective-permute-start(f32[4,192,256]{2,1,0:T(8,128)} %get-tuple-element.49), channel_id=1, source_target_pairs={{0,32},{8,40},{16,48},{24,56},{32,64},{40,72},{48,80},{56,88},{64,... | collective-permute-start | bytes 2359304 | tf_op jit(solution)/shard_map/ppermute | solution.py:548
  99.4 0.0 collective-permute-done.last0
  99.5 0.0 collective-permute-start.5
  99.5 0.0 collective-permute-done.1.last1
  99.5 0.1 collective-permute-start.6
  99.5 0.0 collective-permute-done.2.last2
  99.6 2.7 %collective-permute-start.7 = (f32[4,192,256]{2,1,0:T(8,128)}, f32[4,192,256]{2,1,0:T(8,128)}, u32[]{:S(2)}, u32[]{:S(2)}) collective-permute-start(f32[4,192,256]{2,1,0:T(8,128)} %get-tuple-element.52), channel_id=1, source_target_pairs={{0,24},{8,0},{16,8},{24,16},{32,56},{40,32},{48,40},{56,48},{64,88... | collective-permute-start | bytes 2359304 | tf_op jit(solution)/shard_map/ppermute | solution.py:548
  102.2 0.0 collective-permute-done.3.last3
  102.2 13.4 %forward.1 = f32[6144,256]{1,0:T(8,128)} custom-call(s32[288]{0:T(512)} %rows_ref.3, s32[288]{0:T(512)} %cols_ref.3, s32[1]{0:T(128)S(6)} %copy.16.count_ref, s32[2]{0:T(128)} %pad_add_fusion.place_ref, f32[288,128,128]{2,1,0:T(8,128)} %tiles_ref.3, bf16[96,256,256]{2,1,0:T(8,128)(2,1)} %bitcast.8, f32[4,192,256]{2,1,0:T(8,128)} %collective-permute-done.last0, ...), custom_call_target="tpu_custom_call" | custom-call | flops 14495514624 | bytes 62914560 | tf_op jit(solution)/shard_map/forward/pallas_call | solution.py:501
  115.6 0.0 collective-permute-done.4.first0
  115.6 0.0 copy-start
  115.6 0.9 collective-permute-done.5.first1
  116.5 0.0 collective-permute-done.6.first2
  116.5 1.3 collective-permute-done.7.first3
  117.8 0.0 copy-done
  117.8 76.6 %scatter.1 = (f32[768,256]{1,0:T(8,128)}, f32[768,256]{1,0:T(8,128)}, f32[768,256]{1,0:T(8,128)}, f32[256,256]{1,0:T(8,128)}, f32[256,256]{1,0:T(8,128)}, /*index=5*/f32[256,256]{1,0:T(8,128)}, f32[256,256]{1,0:T(8,128)}) custom-call(f32[768,256]{1,0:T(8,128)} %x_in.1, f32[768,256]{1,0:T(8,128)} %c_in.1, f32[256,256]{1,0:T(8,128)} %wq_ref.3, ...), custom_call_target="tpu_custom_call" | custom-call | tf_op jit(solution)/shard_map/scatter/pallas_call | solution.py:758
  194.4 4.3 %finish.1 = (f32[768,256]{1,0:T(8,128)}, f32[768,256]{1,0:T(8,128)}, f32[256,256]{1,0:T(8,128)}, f32[256,256]{1,0:T(8,128)}, f32[256,256]{1,0:T(8,128)}, /*index=5*/f32[256,256]{1,0:T(8,128)}) custom-call(f32[768,256]{1,0:T(8,128)} %get-tuple-element.53.own_hbm, f32[256,256]{1,0:T(8,128)} %wg_ref.3, f32[768,256]{1,0:T(8,128)} %get-tuple-element.54.refs_0_, ...), custom_call_target="tpu_custom_call" | custom-call | tf_op jit(solution)/shard_map/finish/pallas_call | solution.py:810
Async XLA Ops:
  69.9 29.6 %collective-permute-start = (f32[4,192,256]{2,1,0:T(8,128)}, f32[4,192,256]{2,1,0:T(8,128)}, u32[]{:S(2)}, u32[]{:S(2)}) collective-permute-start(f32[4,192,256]{2,1,0:T(8,128)} %get-tuple-element.43), channel_id=1, source_target_pairs={{0,32},{8,40},{16,48},{24,56},{32,64},{40,72},{48,80},{56,88},{64,... | collective-permute-start | bytes 2359304 | tf_op jit(solution)/shard_map/ppermute | solution.py:548
  71.1 28.4 %collective-permute-start.1 = (f32[4,192,256]{2,1,0:T(8,128)}, f32[4,192,256]{2,1,0:T(8,128)}, u32[]{:S(2)}, u32[]{:S(2)}) collective-permute-start(f32[4,192,256]{2,1,0:T(8,128)} %get-tuple-element.44), channel_id=1, source_target_pairs={{0,96},{8,104},{16,112},{24,120},{32,0},{40,8},{48,16},{56,24},{64... | collective-permute-start | bytes 2359304 | tf_op jit(solution)/shard_map/ppermute | solution.py:548
  72.7 26.9 %collective-permute-start.2 = (f32[4,192,256]{2,1,0:T(8,128)}, f32[4,192,256]{2,1,0:T(8,128)}, u32[]{:S(2)}, u32[]{:S(2)}) collective-permute-start(f32[4,192,256]{2,1,0:T(8,128)} %get-tuple-element.45), channel_id=1, source_target_pairs={{0,8},{8,16},{16,24},{24,0},{32,40},{40,48},{48,56},{56,32},{64,72... | collective-permute-start | bytes 2359304 | tf_op jit(solution)/shard_map/ppermute | solution.py:548
  72.7 29.6 %collective-permute-start.3 = (f32[4,192,256]{2,1,0:T(8,128)}, f32[4,192,256]{2,1,0:T(8,128)}, u32[]{:S(2)}, u32[]{:S(2)}) collective-permute-start(f32[4,192,256]{2,1,0:T(8,128)} %get-tuple-element.46), channel_id=1, source_target_pairs={{0,24},{8,0},{16,8},{24,16},{32,56},{40,32},{48,40},{56,48},{64,88... | collective-permute-start | bytes 2359304 | tf_op jit(solution)/shard_map/ppermute | solution.py:548
  90.2 25.4 %collective-permute-start.4 = (f32[4,192,256]{2,1,0:T(8,128)}, f32[4,192,256]{2,1,0:T(8,128)S(1)}, u32[]{:S(2)}, u32[]{:S(2)}) collective-permute-start(f32[4,192,256]{2,1,0:T(8,128)} %get-tuple-element.49), channel_id=1, source_target_pairs={{0,32},{8,40},{16,48},{24,56},{32,64},{40,72},{48,80},{56,88},{64,... | collective-permute-start | bytes 2359304 | tf_op jit(solution)/shard_map/ppermute | solution.py:548
  99.5 17.0 %collective-permute-start.5 = (f32[4,192,256]{2,1,0:T(8,128)}, f32[4,192,256]{2,1,0:T(8,128)}, u32[]{:S(2)}, u32[]{:S(2)}) collective-permute-start(f32[4,192,256]{2,1,0:T(8,128)} %get-tuple-element.50), channel_id=1, source_target_pairs={{0,96},{8,104},{16,112},{24,120},{32,0},{40,8},{48,16},{56,24},{64... | collective-permute-start | bytes 2359304 | tf_op jit(solution)/shard_map/ppermute | solution.py:548
  99.5 17.0 %collective-permute-start.6 = (f32[4,192,256]{2,1,0:T(8,128)}, f32[4,192,256]{2,1,0:T(8,128)}, u32[]{:S(2)}, u32[]{:S(2)}) collective-permute-start(f32[4,192,256]{2,1,0:T(8,128)} %get-tuple-element.51), channel_id=1, source_target_pairs={{0,8},{8,16},{16,24},{24,0},{32,40},{40,48},{48,56},{56,32},{64,72... | collective-permute-start | bytes 2359304 | tf_op jit(solution)/shard_map/ppermute | solution.py:548
  99.6 18.2 %collective-permute-start.7 = (f32[4,192,256]{2,1,0:T(8,128)}, f32[4,192,256]{2,1,0:T(8,128)}, u32[]{:S(2)}, u32[]{:S(2)}) collective-permute-start(f32[4,192,256]{2,1,0:T(8,128)} %get-tuple-element.52), channel_id=1, source_target_pairs={{0,24},{8,0},{16,8},{24,16},{32,56},{40,32},{48,40},{56,48},{64,88... | collective-permute-start | bytes 2359304 | tf_op jit(solution)/shard_map/ppermute | solution.py:548
  115.6 2.2 %copy-start = (f32[4,192,256]{2,1,0:T(8,128)}, f32[4,192,256]{2,1,0:T(8,128)S(1)}, u32[]{:S(2)}) copy-start(f32[4,192,256]{2,1,0:T(8,128)S(1)} %collective-permute-done.4.first0) | copy-start | bytes 2359300

commit v5 on v4

--- a/solution.py
+++ b/solution.py
@@ -387,22 +387,26 @@
     )(x, cot, wq, wk, wv)
 
 
-CHUNK = 32
+CHUNK = 48
 SLOTS = 3
+
+
+def fetch(chunk, slot, tiles_ref, buf, tile_sem):
+    return pltpu.make_async_copy(
+        tiles_ref.at[pl.ds(chunk * CHUNK, CHUNK)], buf.at[slot], tile_sem.at[slot]
+    )
+
+
+def first_tiles(count, *refs):
+    for i in range(SLOTS - 1):
+        @pl.when(i * CHUNK < count)
+        def _(i=i):
+            fetch(i, i, *refs).start()
 
 
 def sweep(count, rows_ref, cols_ref, tiles_ref, buf, tile_sem, body):
     chunks = (count + CHUNK - 1) // CHUNK
-
-    def fetch(chunk, slot):
-        return pltpu.make_async_copy(
-            tiles_ref.at[pl.ds(chunk * CHUNK, CHUNK)], buf.at[slot], tile_sem.at[slot]
-        )
-
-    for i in range(SLOTS - 1):
-        @pl.when(i < chunks)
-        def _(i=i):
-            fetch(i, i).start()
+    refs = (tiles_ref, buf, tile_sem)
 
     @pl.loop(0, chunks)
     def _(chunk):
@@ -410,9 +414,9 @@
 
         @pl.when(chunk + SLOTS - 1 < chunks)
         def _():
-            fetch(chunk + SLOTS - 1, (chunk + SLOTS - 1) % SLOTS).start()
-
-        fetch(chunk, slot).wait()
+            fetch(chunk + SLOTS - 1, (chunk + SLOTS - 1) % SLOTS, *refs).start()
+
+        fetch(chunk, slot, *refs).wait()
         for i in range(CHUNK):
             at = chunk * CHUNK + i
             tile = buf[slot, i]
@@ -435,6 +439,7 @@
     cs, t, buf, sem, tile_sem,
 ):
     load = pltpu.make_async_copy(cs_ref, cs, sem.at[0])
+    first_tiles(count_ref[0], tiles_ref, buf, tile_sem)
     load.start()
     t[...] = jnp.zeros_like(t)
     load.wait()
@@ -467,6 +472,7 @@
         pltpu.make_async_copy(last, late.at[kind], sem.at[1 + kind])
         for kind, last in enumerate((last0, last1, last2, last3))
     ]
+    first_tiles(count_ref[0], tiles_ref, buf, tile_sem)
     for copy in loads + [load]:
         copy.start()
     f[...] = jnp.zeros_like(f)

time: 200 us -> 198 us (0.990)
  starting transfers between devices: 17.5 us -> 14.9 us
  waiting for transfers between devices: 2.2 us -> 0.02 us
    pallas_call x2, Pallas kernels: 27 us -> 32.8 us  [run_sweep(): pl.pallas_call(kernel, out_shape=out_shape, in_specs=[smem] * 4 + [hbm] *...]
    pallas_call x1, Pallas kernels: 76.6 us -> 72 us  [run_scatter(): pl.pallas_call(scatter_kernel, out_shape=[block, block, block, weight, we...]
    ppermute x8, starting transfers between devices: 17.5 us -> 14.9 us  [ring_sends(): sent.append(lax.ppermute(array, 'rows', pairs))]
    ppermute x8, waiting for transfers between devices: 2.2 us -> 0.02 us  [ring_sends(): sent.append(lax.ppermute(array, 'rows', pairs))]
  transfers between devices with their start and end apart: 8 -> 8, of which waited for: 2 -> 0; matrix products, arithmetic and copies ran while one was open for 0% -> 0% of each run, Pallas kernels for 14% -> 17%
where the time goes in v5:
time: 198 us; the launch traced here: 196 us
  Pallas kernels  178 us (90%)
  starting transfers between devices  14.9 us (8%)
    pallas_call x1, Pallas kernels, run_scatter(): pl.pallas_call(scatter_kernel, out_shape=[block, block, block, weight, we...  72 us
    pallas_call x1, Pallas kernels, run_gather(): pl.pallas_call(gather_kernel, out_shape=[jax.ShapeDtypeStruct((16, BLK, 2...  69.2 us
    pallas_call x2, Pallas kernels, run_sweep(): pl.pallas_call(kernel, out_shape=out_shape, in_specs=[smem] * 4 + [hbm] *...  32.8 us
    ppermute x8, starting transfers between devices, ring_sends(): sent.append(lax.ppermute(array, 'rows', pairs))  14.9 us
    pallas_call x1, Pallas kernels, run_finish(): pl.pallas_call(finish_kernel, out_shape=[jax.ShapeDtypeStruct(a.shape, F3...  4.27 us
  transfers between devices with their start and end apart: 8, of which 0 were waited for; matrix products, arithmetic and copies ran while one was open for 0% of the time, Pallas kernels for 17%

profile of v5, /device:TPU:1, one launch (start us, length us, event | category | flops | bytes accessed | tf_op | source)
XLA Modules:
  0.0 196.1 jit_solution(5597319910462732100)
XLA Ops:
  0.6 69.2 %gather.1 = (bf16[16,6,256,256]{3,2,1,0:T(8,128)(2,1)}, bf16[8,6,256,256]{3,2,1,0:T(8,128)(2,1)}, f32[4,192,256]{2,1,0:T(8,128)}, f32[4,192,256]{2,1,0:T(8,128)}...) custom-call(f32[768,256]{1,0:T(8,128)} %x_in.1, ...), custom_call_target="tpu_custom_call" | custom-call | tf_op jit(solution)/shard_map/gather/pallas_call | solution.py:359
  69.9 1.2 collective-permute-start
  71.1 1.6 collective-permute-start.1
  72.7 0.0 collective-permute-start.2
  72.7 2.7 %collective-permute-start.3 = (f32[4,192,256]{2,1,0:T(8,128)}, f32[4,192,256]{2,1,0:T(8,128)}, u32[]{:S(2)}, u32[]{:S(2)}) collective-permute-start(f32[4,192,256]{2,1,0:T(8,128)} %get-tuple-element.46), channel_id=1, source_target_pairs={{0,24},{8,0},{16,8},{24,16},{32,56},{40,32},{48,40},{56,48},{64,88... | collective-permute-start | bytes 2359304 | tf_op jit(solution)/shard_map/ppermute | solution.py:554
  76.0 0.6 pad_add_fusion.place_ref
  76.6 15.9 %backward.1 = (f32[12288,256]{1,0:T(8,128)}, f32[4,192,256]{2,1,0:T(8,128)}, f32[4,192,256]{2,1,0:T(8,128)}, f32[4,192,256]{2,1,0:T(8,128)}, f32[4,192,256]{2,1,0:T(8,128)}) custom-call(s32[288]{0:T(512)} %rows_ref.3, s32[288]{0:T(512)} %cols_ref.3, s32[1]{0:T(128)S(6)} %copy.16.count_ref, s32[2]{0:T(128)} %pad_add_fusion.place_ref, ...), custom_call_target="tpu_custom_call" | custom-call | flops 14495514624 | bytes 62914560 | tf_op jit(solution)/shard_map/backward/pallas_call | solution.py:507
  92.5 0.1 collective-permute-start.4
  92.6 0.0 collective-permute-done.last0
  92.6 2.7 %collective-permute-start.5 = (f32[4,192,256]{2,1,0:T(8,128)}, f32[4,192,256]{2,1,0:T(8,128)}, u32[]{:S(2)}, u32[]{:S(2)}) collective-permute-start(f32[4,192,256]{2,1,0:T(8,128)} %get-tuple-element.50), channel_id=1, source_target_pairs={{0,96},{8,104},{16,112},{24,120},{32,0},{40,8},{48,16},{56,24},{64... | collective-permute-start | bytes 2359304 | tf_op jit(solution)/shard_map/ppermute | solution.py:554
  95.3 0.0 collective-permute-done.1.last1
  95.3 0.0 collective-permute-start.6
  95.3 0.0 collective-permute-done.2.last2
  95.3 6.6 %collective-permute-start.7 = (f32[4,192,256]{2,1,0:T(8,128)}, f32[4,192,256]{2,1,0:T(8,128)}, u32[]{:S(2)}, u32[]{:S(2)}) collective-permute-start(f32[4,192,256]{2,1,0:T(8,128)} %get-tuple-element.52), channel_id=1, source_target_pairs={{0,24},{8,0},{16,8},{24,16},{32,56},{40,32},{48,40},{56,48},{64,88... | collective-permute-start | bytes 2359304 | tf_op jit(solution)/shard_map/ppermute | solution.py:554
  101.9 0.0 collective-permute-done.3.last3
  101.9 16.8 %forward.1 = f32[6144,256]{1,0:T(8,128)} custom-call(s32[288]{0:T(512)} %rows_ref.3, s32[288]{0:T(512)} %cols_ref.3, s32[1]{0:T(128)S(6)} %copy.16.count_ref, s32[2]{0:T(128)} %pad_add_fusion.place_ref, f32[288,128,128]{2,1,0:T(8,128)} %tiles_ref.3, bf16[96,256,256]{2,1,0:T(8,128)(2,1)} %bitcast.8, f32[4,192,256]{2,1,0:T(8,128)} %collective-permute-done.last0, ...), custom_call_target="tpu_custom_call" | custom-call | flops 14495514624 | bytes 62914560 | tf_op jit(solution)/shard_map/forward/pallas_call | solution.py:507
  118.8 0.0 collective-permute-done.4.first0
  118.8 0.0 copy-start
  118.8 0.0 collective-permute-done.5.first1
  118.8 0.0 collective-permute-done.6.first2
  118.8 0.0 collective-permute-done.7.first3
  118.8 0.8 copy-done
  119.7 72.0 %scatter.1 = (f32[768,256]{1,0:T(8,128)}, f32[768,256]{1,0:T(8,128)}, f32[768,256]{1,0:T(8,128)}, f32[256,256]{1,0:T(8,128)}, f32[256,256]{1,0:T(8,128)}, /*index=5*/f32[256,256]{1,0:T(8,128)}, f32[256,256]{1,0:T(8,128)}) custom-call(f32[768,256]{1,0:T(8,128)} %x_in.1, f32[768,256]{1,0:T(8,128)} %c_in.1, f32[256,256]{1,0:T(8,128)} %wq_ref.3, ...), custom_call_target="tpu_custom_call" | custom-call | tf_op jit(solution)/shard_map/scatter/pallas_call | solution.py:764
  191.7 4.3 %finish.1 = (f32[768,256]{1,0:T(8,128)}, f32[768,256]{1,0:T(8,128)}, f32[256,256]{1,0:T(8,128)}, f32[256,256]{1,0:T(8,128)}, f32[256,256]{1,0:T(8,128)}, /*index=5*/f32[256,256]{1,0:T(8,128)}) custom-call(f32[768,256]{1,0:T(8,128)} %get-tuple-element.53.own_hbm, f32[256,256]{1,0:T(8,128)} %wg_ref.3, f32[768,256]{1,0:T(8,128)} %get-tuple-element.54.refs_0_, ...), custom_call_target="tpu_custom_call" | custom-call | tf_op jit(solution)/shard_map/finish/pallas_call | solution.py:816
Async XLA Ops:
  69.9 22.7 %collective-permute-start = (f32[4,192,256]{2,1,0:T(8,128)}, f32[4,192,256]{2,1,0:T(8,128)}, u32[]{:S(2)}, u32[]{:S(2)}) collective-permute-start(f32[4,192,256]{2,1,0:T(8,128)} %get-tuple-element.43), channel_id=1, source_target_pairs={{0,32},{8,40},{16,48},{24,56},{32,64},{40,72},{48,80},{56,88},{64,... | collective-permute-start | bytes 2359304 | tf_op jit(solution)/shard_map/ppermute | solution.py:554
  71.1 24.2 %collective-permute-start.1 = (f32[4,192,256]{2,1,0:T(8,128)}, f32[4,192,256]{2,1,0:T(8,128)}, u32[]{:S(2)}, u32[]{:S(2)}) collective-permute-start(f32[4,192,256]{2,1,0:T(8,128)} %get-tuple-element.44), channel_id=1, source_target_pairs={{0,96},{8,104},{16,112},{24,120},{32,0},{40,8},{48,16},{56,24},{64... | collective-permute-start | bytes 2359304 | tf_op jit(solution)/shard_map/ppermute | solution.py:554
  72.7 22.6 %collective-permute-start.2 = (f32[4,192,256]{2,1,0:T(8,128)}, f32[4,192,256]{2,1,0:T(8,128)}, u32[]{:S(2)}, u32[]{:S(2)}) collective-permute-start(f32[4,192,256]{2,1,0:T(8,128)} %get-tuple-element.45), channel_id=1, source_target_pairs={{0,8},{8,16},{16,24},{24,0},{32,40},{40,48},{48,56},{56,32},{64,72... | collective-permute-start | bytes 2359304 | tf_op jit(solution)/shard_map/ppermute | solution.py:554
  72.7 29.2 %collective-permute-start.3 = (f32[4,192,256]{2,1,0:T(8,128)}, f32[4,192,256]{2,1,0:T(8,128)}, u32[]{:S(2)}, u32[]{:S(2)}) collective-permute-start(f32[4,192,256]{2,1,0:T(8,128)} %get-tuple-element.46), channel_id=1, source_target_pairs={{0,24},{8,0},{16,8},{24,16},{32,56},{40,32},{48,40},{56,48},{64,88... | collective-permute-start | bytes 2359304 | tf_op jit(solution)/shard_map/ppermute | solution.py:554
  92.5 26.3 %collective-permute-start.4 = (f32[4,192,256]{2,1,0:T(8,128)}, f32[4,192,256]{2,1,0:T(8,128)S(1)}, u32[]{:S(2)}, u32[]{:S(2)}) collective-permute-start(f32[4,192,256]{2,1,0:T(8,128)} %get-tuple-element.49), channel_id=1, source_target_pairs={{0,32},{8,40},{16,48},{24,56},{32,64},{40,72},{48,80},{56,88},{64,... | collective-permute-start | bytes 2359304 | tf_op jit(solution)/shard_map/ppermute | solution.py:554
  92.6 26.2 %collective-permute-start.5 = (f32[4,192,256]{2,1,0:T(8,128)}, f32[4,192,256]{2,1,0:T(8,128)}, u32[]{:S(2)}, u32[]{:S(2)}) collective-permute-start(f32[4,192,256]{2,1,0:T(8,128)} %get-tuple-element.50), channel_id=1, source_target_pairs={{0,96},{8,104},{16,112},{24,120},{32,0},{40,8},{48,16},{56,24},{64... | collective-permute-start | bytes 2359304 | tf_op jit(solution)/shard_map/ppermute | solution.py:554
  95.3 23.5 %collective-permute-start.6 = (f32[4,192,256]{2,1,0:T(8,128)}, f32[4,192,256]{2,1,0:T(8,128)}, u32[]{:S(2)}, u32[]{:S(2)}) collective-permute-start(f32[4,192,256]{2,1,0:T(8,128)} %get-tuple-element.51), channel_id=1, source_target_pairs={{0,8},{8,16},{16,24},{24,0},{32,40},{40,48},{48,56},{56,32},{64,72... | collective-permute-start | bytes 2359304 | tf_op jit(solution)/shard_map/ppermute | solution.py:554
  95.3 23.5 %collective-permute-start.7 = (f32[4,192,256]{2,1,0:T(8,128)}, f32[4,192,256]{2,1,0:T(8,128)}, u32[]{:S(2)}, u32[]{:S(2)}) collective-permute-start(f32[4,192,256]{2,1,0:T(8,128)} %get-tuple-element.52), channel_id=1, source_target_pairs={{0,24},{8,0},{16,8},{24,16},{32,56},{40,32},{48,40},{56,48},{64,88... | collective-permute-start | bytes 2359304 | tf_op jit(solution)/shard_map/ppermute | solution.py:554
  118.8 0.9 copy-start
